TPU v7x, 128 devices: a whole 4x4x4 slice. The times are simulated.
128 devices in a mesh: clip: 32 (over z, x, y_lo), group: 4 (over y_hi, core).
Axes of the slice: x: 4, y: 4 (y_hi: 2, y_lo: 2; y = y_hi * 2 + y_lo), z: 4, core: 2. Of those that a mesh axis runs over, the one named last changes fastest.
Arguments:
- clip_frames: bfloat16 [4, 32, 64, 64, 256], P('group', 'clip'), may hold values from -6 to 6
- w_spatial: bfloat16 [3, 3, 256, 256], replicated, may hold values from -0.125 to 0.125
- w_time: bfloat16 [3, 256, 256], replicated, may hold values from -0.21875 to 0.21875
- cotangent: bfloat16 [4, 16, 64, 64, 256], P('group', None, 'clip'), may hold values from -6 to 6
- frame_time: int32 [32], replicated, may hold values from 0 to 31, each once
Outputs:
- clip_grad: bfloat16 [4, 32, 64, 64, 256], P('group', 'clip')
- space_grad: float32 [3, 3, 256, 256], P(None, None, None, 'group')
- time_grad: float32 [3, 256, 256], P(None, None, 'group')
Inputs may be any that keep to these rules, and one draw needn't show every extreme that they name: `frame_time`: each time from 0 to 31 appears exactly once, the same table for every clip.
All inputs are finite; a program needn't handle non-finite values.
Results may differ from a plain program's by a relative error of at most 0.0058.
Values may be sent and summed in bfloat16 or wider, within the bound.
No kernel may reach another device: no remote copies, remote signals or barrier semaphores. Data moves between devices by JAX's collectives and lax.ppermute only.
A program may use at most 128 MiB of HBM per device.

v0:
```python
import math

import jax
import jax.numpy as jnp
import numpy as np
from jax import lax
from jax.sharding import PartitionSpec as P


def conv_forward(frames, weight):
    height = frames.shape[1]
    col_count = frames.shape[2]
    padded = jnp.pad(frames, ((0, 0), (1, 1), (1, 1), (0, 0)))
    running = jnp.zeros(frames.shape, jnp.float32)
    for row_tap in range(3):
        for col_tap in range(3):
            window = padded[:, row_tap : row_tap + height, col_tap : col_tap + col_count]
            running = running + jnp.einsum(
                "fhwc,cd->fhwd",
                window,
                weight[row_tap, col_tap],
                preferred_element_type=jnp.float32,
            )
    return running


def conv_transpose(grads, weight):
    height = grads.shape[1]
    col_count = grads.shape[2]
    padded = jnp.pad(grads, ((0, 0), (1, 1), (1, 1), (0, 0)))
    running = jnp.zeros(grads.shape, jnp.float32)
    for row_tap in range(3):
        for col_tap in range(3):
            window = padded[
                :, 2 - row_tap : 2 - row_tap + height, 2 - col_tap : 2 - col_tap + col_count
            ]
            running = running + jnp.einsum(
                "fhwd,cd->fhwc",
                window,
                weight[row_tap, col_tap],
                preferred_element_type=jnp.float32,
            )
    return running


def filter_grad(frames, grads):
    height = frames.shape[1]
    col_count = frames.shape[2]
    padded = jnp.pad(frames, ((0, 0), (1, 1), (1, 1), (0, 0)))
    rows_out = []
    for row_tap in range(3):
        taps = []
        for col_tap in range(3):
            window = padded[:, row_tap : row_tap + height, col_tap : col_tap + col_count]
            taps.append(
                jnp.einsum("fhwc,fhwd->cd", window, grads, preferred_element_type=jnp.float32)
            )
        rows_out.append(jnp.stack(taps))
    return jnp.stack(rows_out)


def silu_slope(values):
    sig = jax.nn.sigmoid(values)
    return sig * (1.0 + values * (1.0 - sig))


def time_tables(frame_count, half_count):
    places = np.arange(frame_count)
    lead_index = places // 2
    odd_flag = places % 2 == 1
    trail_index = np.minimum((places + 1) // 2, half_count - 1)
    trail_valid = odd_flag & ((places + 1) // 2 < half_count) | (places == 0)
    even_mask = (~odd_flag).astype(np.float32)
    return (lead_index, trail_index, trail_valid, even_mask)


def temporal(acts, lead_part, trail_part, w_time, even_mask):
    w_lead = jnp.where(even_mask[:, None, None] > 0.5, w_time[1], w_time[2])
    grads = jnp.einsum("fhwd,fcd->fhwc", lead_part, w_lead, preferred_element_type=jnp.float32)
    grads = grads + jnp.einsum(
        "fhwd,cd->fhwc", trail_part, w_time[0], preferred_element_type=jnp.float32
    )
    per_frame = jnp.einsum("fhwc,fhwd->fcd", acts, lead_part, preferred_element_type=jnp.float32)
    grad_one = jnp.einsum("f,fcd->cd", even_mask, per_frame)
    grad_two = jnp.einsum("f,fcd->cd", 1.0 - even_mask, per_frame)
    grad_zero = jnp.einsum("fhwc,fhwd->cd", acts, trail_part, preferred_element_type=jnp.float32)
    return (grads.astype(jnp.bfloat16), jnp.stack([grad_zero, grad_one, grad_two]))


def local(clip_frames, w_spatial, w_time, cotangent, frame_time):
    frames = clip_frames[0]
    frame_count = frame_time.shape[0]
    half_count = frame_count // 2
    hidden = conv_forward(frames, w_spatial)
    acts = jax.nn.silu(hidden).astype(jnp.bfloat16)
    cotan = cotangent[0]
    lead_index, trail_index, trail_valid, even_np = time_tables(frame_count, half_count)
    lead_part = cotan[jnp.asarray(lead_index, jnp.int32)]
    trail_part = jnp.where(
        jnp.asarray(trail_valid)[:, None, None, None],
        cotan[jnp.asarray(trail_index, jnp.int32)],
        jnp.zeros((), jnp.bfloat16),
    )
    rows_acts = lax.all_to_all(acts, "clip", split_axis=1, concat_axis=0, tiled=True)
    positions = jnp.arange(frame_count, dtype=jnp.int32)
    matches = frame_time[None, :] == positions[:, None]
    inverse = jnp.sum(jnp.where(matches, positions[None, :], 0), axis=1)
    acts_time = jnp.take(rows_acts, inverse, axis=0)
    even_mask = jnp.asarray(even_np, jnp.float32)
    grad_time, wt_grad = temporal(acts_time, lead_part, trail_part, w_time, even_mask)
    grad_store = jnp.take(grad_time, frame_time, axis=0)
    grad_acts = lax.all_to_all(grad_store, "clip", split_axis=0, concat_axis=1, tiled=True)
    hidden_grad = (grad_acts.astype(jnp.float32) * silu_slope(hidden)).astype(jnp.bfloat16)
    ws_grad = filter_grad(frames, hidden_grad)
    clip_grad = conv_transpose(hidden_grad, w_spatial).astype(jnp.bfloat16)
    summed = lax.psum((ws_grad, wt_grad), "clip")
    ws_total, wt_total = (
        lax.psum_scatter(summed[0], "group", scatter_dimension=3, tiled=True),
        lax.psum_scatter(summed[1], "group", scatter_dimension=2, tiled=True),
    )
    clip_total = clip_frames.shape[0] * lax.axis_size("group")
    factor = 1.0 / math.sqrt(clip_total * frame_count * frames.shape[1] * frames.shape[2])
    return (clip_grad[None], ws_total * factor, wt_total * factor)


def solution(mesh):
    return jax.shard_map(
        local,
        mesh=mesh,
        in_specs=(
            P("group", "clip", None, None, None),
            P(),
            P(),
            P("group", None, "clip", None, None),
            P(),
        ),
        out_specs=(
            P("group", "clip", None, None, None),
            P(None, None, None, "group"),
            P(None, None, "group"),
        ),
        check_vma=False,
    )
```

profile of v0, /device:TPU:0, one launch (start us, length us, event | category | flops | bytes accessed | tf_op | source)
XLA Modules:
  0.0 547.0 jit_solution(2070241255901003899)
XLA Ops:
  7.2 0.7 compare_select_fusion.1
  7.9 0.7 compare_and_fusion.1
  8.6 0.7 pad_clamp_fusion.3
  9.2 1.0 slice_bitcast_fusion.1
  10.2 0.7 pad_clamp_fusion.2
  10.9 2.0 gather_fusion
  12.9 0.7 gather_fusion.1
  13.6 3.9 fusion.5
  17.6 3.0 add_convert_fusion.1
  20.6 2.3 gather_fusion.2
  22.8 1.6 broadcast_select_fusion.2
  24.4 9.7 %all-to-all-start = ((bf16[32,2,64,256]{3,2,1,0:T(8,128)(2,1)}), bf16[32,2,64,256]{3,2,1,0:T(8,128)(2,1)}, u32[]{:S(2)}, u32[]{:S(2)}) async-start(bf16[32,2,64,256]{3,2,1,0:T(8,128)(2,1)} %broadcast_select_fusion.2), calls=%async_computation | async-start | bytes 4194304 | tf_op jit(solution)/shard_map/all_to_all | solution.py:112
  34.1 3.7 fusion.29
  37.8 2.7 fusion.33
  40.5 0.1 select_reduce_fusion
  40.7 2.7 fusion.37
  43.4 2.7 fusion.45
  46.1 2.7 fusion.49
  48.8 2.7 fusion.53
  51.5 2.7 fusion.57
  54.2 2.7 fusion.41
  56.8 7.3 %all-to-all-done = bf16[32,2,64,256]{3,2,1,0:T(8,128)(2,1)} async-done(((bf16[32,2,64,256]{3,2,1,0:T(8,128)(2,1)}), bf16[32,2,64,256]{3,2,1,0:T(8,128)(2,1)}, u32[]{:S(2)}, u32[]{:S(2)}) %all-to-all-start) | async-done | bytes 2097184 | tf_op jit(solution)/shard_map/all_to_all | solution.py:112
  64.1 15.0 %fusion.69 = (bf16[1,64,64,256]{3,2,0,1:T(8,128)(2,1)}, bf16[64,64,256]{2,1,0:T(8,128)(2,1)S(1)}) fusion(bf16[32,2,64,256]{3,2,1,0:T(8,128)(2,1)} %all-to-all-done, bf16[3,3,256,256]{3,2,1,0:T(8,128)(2,1)} %param.12, bf16[1,64,64,256]{3,2,1,0:T(8,128)(2,1)} %bitcast.259, f32[64,64,256]{2,1,0:T(8,128)} %fusion.29, f32[64,64,256]{2,1,0:T(8,128)} %fusion.33, ...), kind=kOutput, calls=%fused_computation.81 | convolution fusion | flops 557842432 | bytes 42074112 | tf_op jit(solution)/shard_map/fhwc,cd->fhwd/dot_general | solution.py:18
  79.2 0.8 fusion.100
  79.9 0.8 fusion.115
  80.7 1.5 fusion.118
  82.2 1.5 fusion.121
  83.6 4.8 all-to-all-start.1
  88.4 0.3 all-reduce.11.cloned.1.call-start
  88.7 2.7 fusion.109
  91.5 0.7 fusion.103
  92.2 0.8 fusion.106
  93.0 0.7 fusion.112
  93.8 0.8 fusion.97
  94.5 0.1 maximum_bitcast_fusion
  94.6 1.6 pad_maximum_fusion
  96.2 4.5 copy.22
  100.8 16.5 %all-to-all-done.1 = bf16[1,64,64,256]{3,2,0,1:T(8,128)(2,1)} async-done(((bf16[1,64,64,256]{3,2,0,1:T(8,128)(2,1)}), bf16[1,64,64,256]{3,2,0,1:T(8,128)(2,1)}, u32[]{:S(2)}, u32[]{:S(2)}) %all-to-all-start.1) | async-done | bytes 2097184 | tf_op jit(solution)/shard_map/all_to_all | solution.py:104
  117.2 3.6 gather_fusion.3
  120.8 4.8 convolution_bitcast_fusion
  125.6 1.2 convolution_bitcast_fusion.1
  126.8 2.4 fusion.2
  129.3 2.4 fusion
  131.8 1.3 copy.24
  133.1 0.3 all-reduce.9.cloned.1.call-start
  133.4 0.3 copy-done.16
  133.7 0.6 dynamic-slice
  135.0 3.7 fusion.10
  138.7 2.9 fusion.12
  141.6 2.7 fusion.14
  144.3 2.7 fusion.16
  147.0 2.8 fusion.18
  149.8 2.7 fusion.20
  152.5 2.7 fusion.22
  155.2 2.7 fusion.151
  157.9 66.9 %all-reduce.11.cloned.1.call-done = (f32[3,3,256,256]{2,1,0,3:T(4,128)}, f32[3,256,256]{1,0,2:T(4,128)}) async-done(((f32[3,3,256,256]{2,1,0,3:T(4,128)}, f32[3,256,256]{1,0,2:T(4,128)}), (f32[3,3,256,256]{2,1,0,3:T(4,128)}, f32[3,256,256]{1,0,2:T(4,128)})) %all-reduce.11.cloned.1.call-update) | async-done | bytes 3145744
  224.8 2.2 constant_dynamic-slice_fusion.1
  227.0 1.7 constant_dynamic-slice_fusion
  228.7 13.2 %fusion.86 = bf16[1,1,64,64,256]{4,3,2,1,0:T(8,128)(2,1)} fusion(f32[64,64,256]{2,1,0:T(8,128)} %fusion.10, f32[64,64,256]{2,1,0:T(8,128)} %fusion.12, f32[64,64,256]{2,1,0:T(8,128)} %fusion.14, f32[64,64,256]{2,1,0:T(8,128)} %fusion.151, f32[64,64,256]{2,1,0:T(8,128)} %fusion.16, f32[64,64,256]{2,1,0:T(8,128)} %fusion.18, f32[64,64,256]{2,1,0:T(8,128)} %fusion.22, ...), kind=kOutput, calls=%fused_computation.101 | convolution fusion | flops 546308096 | bytes 37879808 | tf_op jit(solution)/shard_map/fhwd,cd->fhwc/dot_general | solution.py:37
  241.9 295.2 %all-reduce.9.cloned.1.call-done = (f32[3,3,256,64]{2,1,0,3:T(4,128)}, f32[3,256,64]{1,0,2:T(4,128)}) async-done(((f32[3,3,256,64]{2,1,0,3:T(4,128)}, f32[3,256,64]{1,0,2:T(4,128)}), (f32[3,3,256,64]{2,1,0,3:T(4,128)}, f32[3,256,64]{1,0,2:T(4,128)})) %all-reduce.9.cloned.1.call-update) | async-done | bytes 786448 | tf_op jit(solution)/shard_map/psum | solution.py:116
  537.1 1.4 broadcast_multiply_fusion
  538.5 0.9 copy.25
  539.4 0.1 broadcast_multiply_fusion.1
  539.5 0.7 copy.26
  (47 shorter events, 0.3 us)
Async XLA Ops:
  7.2 3.7 copy-start
  12.9 0.7 copy-start.18
  13.6 4.0 copy-start.5
  13.6 3.9 copy-start.14
  24.4 9.7 %copy-start.2 = (bf16[1,1,64,64,256]{4,3,2,1,0:T(8,128)(2,1)S(1)}, bf16[1,1,64,64,256]{4,3,2,1,0:T(8,128)(2,1)}, u32[]{:S(2)}) copy-start(bf16[1,1,64,64,256]{4,3,2,1,0:T(8,128)(2,1)} %param.11) | copy-start | bytes 6291460
  24.4 39.7 %all-to-all-start = ((bf16[32,2,64,256]{3,2,1,0:T(8,128)(2,1)}), bf16[32,2,64,256]{3,2,1,0:T(8,128)(2,1)}, u32[]{:S(2)}, u32[]{:S(2)}) async-start(bf16[32,2,64,256]{3,2,1,0:T(8,128)(2,1)} %broadcast_select_fusion.2), calls=%async_computation | async-start | bytes 4194304 | tf_op jit(solution)/shard_map/all_to_all | solution.py:112
  34.1 3.7 copy-start.8
  37.8 2.7 copy-start.15
  64.1 15.0 %copy-start.3 = (bf16[1,1,64,64,256]{4,3,2,1,0:T(8,128)(2,1)S(1)}, bf16[1,1,64,64,256]{4,3,2,1,0:T(8,128)(2,1)}, u32[]{:S(2)}) copy-start(bf16[1,1,64,64,256]{4,3,2,1,0:T(8,128)(2,1)} %param.11) | copy-start | bytes 6291460
  83.6 33.6 %all-to-all-start.1 = ((bf16[1,64,64,256]{3,2,0,1:T(8,128)(2,1)}), bf16[1,64,64,256]{3,2,0,1:T(8,128)(2,1)}, u32[]{:S(2)}, u32[]{:S(2)}) async-start(bf16[1,64,64,256]{3,2,0,1:T(8,128)(2,1)} %get-tuple-element.17), calls=%async_computation.1 | async-start | bytes 4194304 | tf_op jit(solution)/shard_map/all_to_all | solution.py:104
  88.4 136.4 %all-reduce.11.cloned.1.call-start = ((), (), s32[]{:S(2)}) async-start(), calls=%async_computation.3 | async-start | bytes 8388608
  88.7 2.7 copy-start.11
  88.7 2.7 copy-start.12
  88.7 2.8 copy-start.4
  120.8 4.8 copy-start.6
  120.8 4.8 copy-start.7
  125.6 1.2 copy-start.17
  126.8 2.5 copy-start.13
  133.1 0.7 copy-start.16
  133.1 404.0 %all-reduce.9.cloned.1.call-start = ((), (), s32[]{:S(2)}) async-start(), calls=%async_computation.2 | async-start | bytes 2097152 | tf_op jit(solution)/shard_map/psum | solution.py:116
  135.0 3.7 copy-start.9
  228.7 311.5 %copy-start.1 = (bf16[1,16,2,64,256]{4,3,2,1,0:T(8,128)(2,1)S(1)}, bf16[1,16,2,64,256]{4,3,2,1,0:T(8,128)(2,1)}, u32[]{:S(2)}) copy-start(bf16[1,16,2,64,256]{4,3,2,1,0:T(8,128)(2,1)} %param.14) | copy-start | bytes 3145732
  537.1 2.3 copy-start.10
Sparse Core Ops, SparseCore 0:
  133.2 91.5 all-reduce.10
  228.8 308.2 all-reduce.8
where the time goes:
time: 548 us; the launch traced here: 547 us
  waiting for transfers between devices  386 us (70%)
  matrix products  101 us (18%)
  local copies, waits for them, and re-layouts  21.9 us (4%)
  between operations  15.1 us (3%)
  starting transfers between devices  15 us (3%)
  other arithmetic  7.69 us (1%)
    psum x1, waiting for transfers between devices, local(): summed = lax.psum((ws_grad, wt_grad), 'clip')  295 us
    unnamed x3, waiting for transfers between devices  66.9 us
    dot_general x9, matrix products, conv_forward(): jnp.einsum('fhwc,cd->fhwd', window, weight[row_tap, col_tap], preferred_e...  37.6 us
    dot_general x9, matrix products, conv_transpose(): jnp.einsum('fhwd,cd->fhwc', window, weight[row_tap, col_tap], preferred_e...  36.1 us
    all_to_all x1, waiting for transfers between devices, local(): lax.all_to_all(acts, 'clip', split_axis=1, concat_axis=0, tiled=True)  16.5 us
  transfers between devices with their start and end apart: 4, of which 4 were waited for; matrix products, arithmetic and copies ran while one was open for 13% of the time, Pallas kernels for 0%

commit v1 on v0

v1 whole, which is shorter than its diff:
```python
import functools
import math

import jax
import jax.numpy as jnp
from jax import lax
from jax.experimental import pallas as pl
from jax.experimental.pallas import tpu as pltpu
from jax.sharding import PartitionSpec as P

BF16 = jnp.bfloat16
F32 = jnp.float32
VMEM_LIMIT = 48 * 1024 * 1024
BOTH = ("clip", "group")


def dot(a, b, dims=((1,), (0,))):
    return lax.dot_general(a, b, (dims, ((), ())), preferred_element_type=F32)


def params():
    return pltpu.CompilerParams(vmem_limit_bytes=VMEM_LIMIT)


def vmem():
    return pl.BlockSpec(memory_space=pltpu.VMEM)


def smem():
    return pl.BlockSpec(memory_space=pltpu.SMEM)


def cost(flops, nbytes, trans=0):
    return pl.CostEstimate(flops=flops, bytes_accessed=nbytes, transcendentals=trans)


def place_of_time(frame_time, inverse):
    def put(s, carry):
        inverse[frame_time[s]] = s
        return carry

    lax.fori_loop(0, frame_time.shape[0], put, 0)


def time_grad_kernel(frame_time, cot, w_time, out, inverse):
    half, pixels, chans = cot.shape
    place_of_time(frame_time, inverse)
    span = min(4, half)
    across = ((1,), (1,))
    for first in range(0, half, span):
        here = cot[first : first + span].reshape(span * pixels, chans)
        even = dot(here, w_time[1], across)
        odd = dot(here, w_time[2], across)
        if first + span < half:
            after = cot[first + 1 : first + span + 1].reshape(span * pixels, chans)
        else:
            after = jnp.concatenate(
                [cot[first + 1 : half].reshape((span - 1) * pixels, chans), jnp.zeros((pixels, chans), BF16)]
            )
        odd = odd + dot(after, w_time[0], across)
        for k in range(span):
            part = even[k * pixels : (k + 1) * pixels]
            if first + k == 0:
                part = part + dot(cot[0], w_time[0], across)
            out[inverse[2 * (first + k)]] = part.astype(BF16)
            out[inverse[2 * (first + k) + 1]] = odd[k * pixels : (k + 1) * pixels].astype(BF16)


def time_grad_call(frame_time, cot, w_time):
    half, pixels, chans = cot.shape
    count = frame_time.shape[0]
    return pl.pallas_call(
        time_grad_kernel,
        out_shape=jax.ShapeDtypeStruct((count, pixels, chans), BF16),
        in_specs=[smem(), vmem(), vmem()],
        out_specs=vmem(),
        scratch_shapes=[pltpu.SMEM((count,), jnp.int32)],
        compiler_params=params(),
        cost_estimate=cost(6 * half * pixels * chans * chans, 4 * count * pixels * chans),
        name="time_grad",
    )(frame_time, cot, w_time)


def side_by_side(block, width):
    rows, chans = block.shape
    wide = block.astype(F32)
    col = lax.rem(lax.broadcasted_iota(jnp.int32, (rows, chans), 0), width)
    left = jnp.where(col == 0, 0.0, pltpu.roll(wide, 1, 0)).astype(BF16)
    right = jnp.where(col == width - 1, 0.0, pltpu.roll(wide, rows - 1, 0)).astype(BF16)
    return left, block, right


def store_cat(cat, start, block, width):
    rows, chans = block.shape
    for j, part in enumerate(side_by_side(block, width)):
        cat[pl.ds(start, rows), j * chans : (j + 1) * chans] = part


def forward_kernel(width, x, w, acts, slope, cat):
    step = pl.program_id(0)
    pixels, chans = x.shape
    rows = acts.shape[0]

    @pl.when(step == 0)
    def _():
        cat[0:width] = jnp.zeros((width, 3 * chans), BF16)
        cat[width + pixels :] = jnp.zeros((width, 3 * chans), BF16)

        def fill(k, carry):
            at = pl.multiple_of(k * rows, rows)
            store_cat(cat, width + at, x[pl.ds(at, rows)], width)
            return carry

        lax.fori_loop(0, pixels // rows, fill, 0)

    at = pl.multiple_of(step * rows, rows)
    hidden = dot(cat[pl.ds(at, rows)], w[0])
    hidden = hidden + dot(cat[pl.ds(at + width, rows)], w[1])
    hidden = hidden + dot(cat[pl.ds(at + 2 * width, rows)], w[2])
    sig = 1.0 / (1.0 + jnp.exp(-hidden))
    acts[...] = (hidden * sig).astype(BF16)
    slope[...] = sig * (1.0 + hidden * (1.0 - sig))


def forward_call(x, w, width, steps=8):
    pixels, chans = x.shape
    rows = pixels // steps
    whole = lambda shape: pl.BlockSpec(shape, lambda k: (0,) * len(shape))
    tile = pl.BlockSpec((rows, chans), lambda k: (k, 0))
    return pl.pallas_call(
        functools.partial(forward_kernel, width),
        grid=(steps,),
        out_shape=(jax.ShapeDtypeStruct((pixels, chans), BF16), jax.ShapeDtypeStruct((pixels, chans), F32)),
        in_specs=[whole(x.shape), whole(w.shape)],
        out_specs=(tile, tile),
        scratch_shapes=[pltpu.VMEM((pixels + 2 * width, 3 * chans), BF16)],
        compiler_params=params(),
        cost_estimate=cost(18 * pixels * chans * chans, 8 * pixels * chans, 2 * pixels * chans),
        name="spatial_forward",
    )(x, w)


def filter_kernel(width, grad, slope, xt, hidden_grad, ws, cat, total):
    step = pl.program_id(0)
    last = pl.num_programs(0) - 1
    rows, chans = grad.shape
    pixels = rows * last

    @pl.when(step == 0)
    def _():
        cat[0:width] = jnp.zeros((width, 3 * chans), BF16)
        cat[width + pixels :] = jnp.zeros((width, 3 * chans), BF16)
        total[...] = jnp.zeros_like(total)

    @pl.when(step < last)
    def _():
        at = pl.multiple_of(step * rows, rows)
        block = (grad[...].astype(F32) * slope[...]).astype(BF16)
        hidden_grad[...] = block
        store_cat(cat, width + at, block, width)

    @pl.when(step > 0)
    def _():
        at = pl.multiple_of((step - 1) * rows, rows)
        for i in range(3):
            total[i] += dot(xt[...], cat[pl.ds(at + (2 - i) * width, rows)])

    @pl.when(step == last)
    def _():
        for i in range(3):
            for j in range(3):
                ws[i, j] = total[i, :, (2 - j) * chans : (3 - j) * chans].T


def filter_call(grad, slope, xt, width, steps=8):
    pixels, chans = grad.shape
    rows = pixels // steps
    tile = pl.BlockSpec((rows, chans), lambda k: (jnp.minimum(k, steps - 1), 0))
    return pl.pallas_call(
        functools.partial(filter_kernel, width),
        grid=(steps + 1,),
        out_shape=(
            jax.ShapeDtypeStruct((pixels, chans), BF16),
            jax.ShapeDtypeStruct((3, 3, chans, chans), F32),
        ),
        in_specs=[tile, tile, pl.BlockSpec((chans, rows), lambda k: (0, jnp.maximum(k - 1, 0)))],
        out_specs=(tile, pl.BlockSpec((3, 3, chans, chans), lambda k: (0, 0, 0, 0))),
        scratch_shapes=[
            pltpu.VMEM((pixels + 2 * width, 3 * chans), BF16),
            pltpu.VMEM((3, chans, 3 * chans), F32),
        ],
        compiler_params=params(),
        cost_estimate=cost(18 * pixels * chans * chans, 12 * pixels * chans),
        name="spatial_filter",
    )(grad, slope, xt)


def back_kernel(width, hidden_grad, w, out, cat):
    step = pl.program_id(0)
    pixels, chans = hidden_grad.shape
    rows = out.shape[0]

    @pl.when(step == 0)
    def _():
        cat[0:width] = jnp.zeros((width, 3 * chans), BF16)
        cat[width + pixels :] = jnp.zeros((width, 3 * chans), BF16)

        def fill(k, carry):
            at = pl.multiple_of(k * rows, rows)
            store_cat(cat, width + at, hidden_grad[pl.ds(at, rows)], width)
            return carry

        lax.fori_loop(0, pixels // rows, fill, 0)

    at = pl.multiple_of(step * rows, rows)
    total = dot(cat[pl.ds(at, rows)], w[0])
    total = total + dot(cat[pl.ds(at + width, rows)], w[1])
    total = total + dot(cat[pl.ds(at + 2 * width, rows)], w[2])
    out[...] = total.astype(BF16)


def back_call(hidden_grad, w, width, steps=8):
    pixels, chans = hidden_grad.shape
    rows = pixels // steps
    whole = lambda shape: pl.BlockSpec(shape, lambda k: (0,) * len(shape))
    return pl.pallas_call(
        functools.partial(back_kernel, width),
        grid=(steps,),
        out_shape=jax.ShapeDtypeStruct((pixels, chans), BF16),
        in_specs=[whole(hidden_grad.shape), whole(w.shape)],
        out_specs=pl.BlockSpec((rows, chans), lambda k: (k, 0)),
        scratch_shapes=[pltpu.VMEM((pixels + 2 * width, 3 * chans), BF16)],
        compiler_params=params(),
        cost_estimate=cost(18 * pixels * chans * chans, 4 * pixels * chans),
        name="spatial_back",
    )(hidden_grad, w)


def time_filter_kernel(frame_time, acts, cot_t, wt, inverse):
    count, pixels, chans = acts.shape
    half = count // 2
    place_of_time(frame_time, inverse)
    first = acts[inverse[0]]
    totals = [dot(cot_t[:, 0:pixels], first), None, None]
    totals[1] = totals[0]
    for u in range(half):
        here = cot_t[:, u * pixels : (u + 1) * pixels]
        if u > 0:
            totals[1] = totals[1] + dot(here, acts[inverse[2 * u]])
        odd = acts[inverse[2 * u + 1]]
        term = dot(here, odd)
        totals[2] = term if totals[2] is None else totals[2] + term
        if u + 1 < half:
            totals[0] = totals[0] + dot(cot_t[:, (u + 1) * pixels : (u + 2) * pixels], odd)
    for k in range(3):
        wt[k] = totals[k]


def time_filter_call(frame_time, acts, cot_t):
    count, pixels, chans = acts.shape
    return pl.pallas_call(
        time_filter_kernel,
        out_shape=jax.ShapeDtypeStruct((3, chans, chans), F32),
        in_specs=[smem(), vmem(), vmem()],
        out_specs=vmem(),
        scratch_shapes=[pltpu.SMEM((count,), jnp.int32)],
        compiler_params=params(),
        cost_estimate=cost(3 * count * pixels * chans * chans, 3 * count * pixels * chans),
        name="time_filter",
    )(frame_time, acts, cot_t)


def exchange(x, axes):
    return lax.all_to_all(x, axes, split_axis=0, concat_axis=0, tiled=True)


def local(clip_frames, w_spatial, w_time, cotangent, frame_time):
    count = frame_time.shape[0]
    height, width, chans = clip_frames.shape[2:]
    clips = lax.axis_size("clip")
    groups = lax.axis_size("group")
    share = chans // groups
    x = clip_frames.reshape(height * width, chans)
    cot = cotangent.reshape(count // 2, -1, chans)

    grad = exchange(time_grad_call(frame_time, cot, w_time), "clip")
    acts, slope = forward_call(x, w_spatial.reshape(3, 3 * chans, chans), width)
    rows_acts = exchange(acts.reshape(count, -1, chans), "clip")
    w_back = w_spatial[::-1, ::-1].transpose(0, 1, 3, 2).reshape(3, 3 * chans, chans)
    hidden_grad, ws = filter_call(grad.reshape(height * width, chans), slope, x.T, width)
    clip_grad = back_call(hidden_grad, w_back, width)
    wt = time_filter_call(frame_time, rows_acts, cot.transpose(2, 0, 1).reshape(chans, -1))

    parts = jnp.concatenate([ws.reshape(9, chans, chans), wt]).astype(BF16)
    taps = parts.shape[0]
    depth = taps * share // clips
    parts = parts.reshape(taps, groups, share, chans).transpose(1, 0, 2, 3)
    parts = parts.reshape(groups, clips, depth, chans).transpose(1, 0, 2, 3)
    parts = exchange(parts.reshape(clips * groups, depth, chans), BOTH)
    clip_total = clip_frames.shape[0] * groups
    factor = 1.0 / math.sqrt(clip_total * count * height * width)
    mine = (jnp.sum(parts.astype(F32), axis=0) * factor).astype(BF16)
    full = exchange(jnp.broadcast_to(mine[None], (clips, depth, chans)), "clip")
    full = full.reshape(taps, share, chans).transpose(0, 2, 1).astype(F32)
    return (clip_grad.reshape(clip_frames.shape), full[:9].reshape(3, 3, chans, share), full[9:])


def solution(mesh):
    return jax.shard_map(
        local,
        mesh=mesh,
        in_specs=(
            P("group", "clip", None, None, None),
            P(),
            P(),
            P("group", None, "clip", None, None),
            P(),
        ),
        out_specs=(
            P("group", "clip", None, None, None),
            P(None, None, None, "group"),
            P(None, None, "group"),
        ),
        check_vma=False,
    )
```

time: 548 us -> 138 us (0.25)
  waiting for transfers between devices: 386 us -> 52.9 us
  matrix products: 101 us -> 0 us
  Pallas kernels: 0 us -> 35 us
  between operations: 15.1 us -> 0.79 us
  starting transfers between devices: 15 us -> 25.8 us
    psum x1 -> x0, waiting for transfers between devices: 295 us -> none  [local(): summed = lax.psum((ws_grad, wt_grad), 'clip')]
    dot_general x33 -> x0, matrix products: 101 us -> none  [the longest x9 37.6 us: conv_forward(): jnp.einsum('fhwc,cd->fhwd', window, weight[row_tap, col_tap], preferred_e...]
    unnamed x3 -> x0, waiting for transfers between devices: 66.9 us -> none
    pallas_call x0 -> x5, Pallas kernels: none -> 35 us  [the longest x1 12 us: filter_call(): pl.pallas_call(functools.partial(filter_kernel, width), grid=(steps + 1,)...]
    all_to_all x2 -> x4, waiting for transfers between devices: 23.8 us -> 52.9 us  [exchange(): return lax.all_to_all(x, axes, split_axis=0, concat_axis=0, tiled=True)]
    all_to_all x2 -> x4, starting transfers between devices: 14.5 us -> 25.8 us  [exchange(): return lax.all_to_all(x, axes, split_axis=0, concat_axis=0, tiled=True)]
    gather x4 -> x0, local copies, waits for them, and re-layouts: 8.55 us -> none  [the longest x1 3.6 us: local(): acts_time = jnp.take(rows_acts, inverse, axis=0)]
    another operation x2 -> x0, local copies, waits for them, and re-layouts: 5.83 us -> none  [the longest x1 4.52 us: filter_grad(): return jnp.stack(rows_out)]
  transfers between devices with their start and end apart: 4 -> 4, of which waited for: 4 -> 4; matrix products, arithmetic and copies ran while one was open for 13% -> 7% of each run, Pallas kernels for 0% -> 21%
where the time goes in v1:
time: 138 us; the launch traced here: 137 us
  waiting for transfers between devices  52.9 us (38%)
  Pallas kernels  35 us (25%)
  starting transfers between devices  25.8 us (19%)
  local copies, waits for them, and re-layouts  17 us (12%)
  other arithmetic  5.85 us (4%)
    all_to_all x4, waiting for transfers between devices, exchange(): return lax.all_to_all(x, axes, split_axis=0, concat_axis=0, tiled=True)  52.9 us
    all_to_all x4, starting transfers between devices, exchange(): return lax.all_to_all(x, axes, split_axis=0, concat_axis=0, tiled=True)  25.8 us
    pallas_call x1, Pallas kernels, filter_call(): pl.pallas_call(functools.partial(filter_kernel, width), grid=(steps + 1,)...  12 us
    pallas_call x1, Pallas kernels, forward_call(): pl.pallas_call(functools.partial(forward_kernel, width), grid=(steps,), o...  8.93 us
    pallas_call x1, Pallas kernels, back_call(): pl.pallas_call(functools.partial(back_kernel, width), grid=(steps,), out_...  8.22 us
    unnamed x26, local copies, waits for them, and re-layouts  6.84 us
    reshape x1, local copies, waits for them, and re-layouts, local(): x = clip_frames.reshape(height * width, chans)  4.16 us
    pallas_call x1, Pallas kernels, time_grad_call(): pl.pallas_call(time_grad_kernel, out_shape=jax.ShapeDtypeStruct((count, p...  3.21 us
  transfers between devices with their start and end apart: 4, of which 4 were waited for; matrix products, arithmetic and copies ran while one was open for 7% of the time, Pallas kernels for 21%

profile of v1, /device:TPU:0, one launch (start us, length us, event | category | flops | bytes accessed | tf_op | source)
XLA Modules:
  0.0 137.3 jit_solution(6766491299629463378)
XLA Ops:
  0.6 0.0 copy-start
  0.6 1.2 copy-done
  1.9 0.0 copy-start.7
  1.9 1.0 copy-done.7
  2.9 0.0 copy-start.8
  2.9 0.7 copy-done.8
  3.5 3.2 %time_grad.1 = bf16[32,128,256]{2,1,0:T(8,128)(2,1)} custom-call(s32[32]{0:T(128)S(1)} %copy-done.8, bf16[16,128,256]{2,1,0:T(8,128)(2,1)S(1)} %bitcast.27, bf16[3,256,256]{2,1,0:T(8,128)(2,1)S(1)} %copy-done.7), custom_call_target="tpu_custom_call" | custom-call | flops 805306368 | bytes 4194304 | tf_op jit(solution)/shard_map/time_grad/pallas_call | solution.py:72
  6.7 0.0 copy-start.3
  6.7 0.0 copy-start.5
  6.7 9.7 %all-to-all-start = ((bf16[32,128,256]{2,1,0:T(8,128)(2,1)}), bf16[32,128,256]{2,1,0:T(8,128)(2,1)}, u32[]{:S(2)}, u32[]{:S(2)}) async-start(bf16[32,128,256]{2,1,0:T(8,128)(2,1)} %time_grad.1), calls=%async_computation | async-start | bytes 4194304 | tf_op jit(solution)/shard_map/all_to_all | solution.py:274
  16.4 0.0 copy-done.3
  16.4 0.0 copy-done.5
  16.4 8.9 %spatial_forward.1 = (bf16[4096,256]{1,0:T(8,128)(2,1)S(1)}, f32[4096,256]{1,0:T(8,128)}) custom-call(bf16[4096,256]{1,0:T(8,128)(2,1)S(1)} %bitcast.30, bf16[3,768,256]{2,1,0:T(8,128)(2,1)S(1)} %bitcast.32), custom_call_target="tpu_custom_call" | custom-call | flops 4831838208 | bytes 8388608 | tf_op jit(solution)/shard_map/spatial_forward/pallas_call | solution.py:130
  25.3 0.0 copy-start.4
  25.3 1.4 %copy-done.4 = bf16[4096,256]{1,0:T(8,128)(2,1)} copy-done((bf16[4096,256]{1,0:T(8,128)(2,1)}, bf16[4096,256]{1,0:T(8,128)(2,1)S(1)}, u32[]{:S(2)}) %copy-start.4) | copy-done | bytes 2097176
  26.7 19.8 %all-to-all-done = bf16[32,128,256]{2,1,0:T(8,128)(2,1)} async-done(((bf16[32,128,256]{2,1,0:T(8,128)(2,1)}), bf16[32,128,256]{2,1,0:T(8,128)(2,1)}, u32[]{:S(2)}, u32[]{:S(2)}) %all-to-all-start) | async-done | bytes 2097184 | tf_op jit(solution)/shard_map/all_to_all | solution.py:274
  46.6 4.0 %all-to-all-start.1 = ((bf16[32,128,256]{2,1,0:T(8,128)(2,1)}), bf16[32,128,256]{2,1,0:T(8,128)(2,1)S(1)}, u32[]{:S(2)}, u32[]{:S(2)}) async-start(bf16[32,128,256]{2,1,0:T(8,128)(2,1)} %bitcast.31), calls=%async_computation.1 | async-start | bytes 4194304 | tf_op jit(solution)/shard_map/all_to_all | solution.py:274
  50.6 0.0 copy-start.1
  50.6 4.2 %copy.12 = bf16[4096,256]{0,1:T(8,128)(2,1)} copy(bf16[4096,256]{1,0:T(8,128)(2,1)} %bitcast.29) | data formatting | bytes 4194304 | tf_op jit(solution)/shard_map/reshape | solution.py:283
  54.8 0.0 copy-done.1
  54.8 1.4 %copy.18.cot_t = bf16[256,2048]{1,0:T(8,128)(2,1)} copy(bf16[256,2048]{0,1:T(8,128)(2,1)S(1)} %bitcast.28) | data formatting | bytes 2097152 | tf_op jit(solution)/shard_map/reshape | solution.py:292
  56.2 12.0 %spatial_filter.1 = (bf16[4096,256]{1,0:T(8,128)(2,1)S(1)}, f32[3,3,256,256]{3,2,1,0:T(8,128)}) custom-call(bf16[4096,256]{1,0:T(8,128)(2,1)} %bitcast.1.grad, f32[4096,256]{1,0:T(8,128)} %get-tuple-element.7.slope, bf16[256,4096]{1,0:T(8,128)(2,1)} %bitcast.36), custom_call_target="tpu_custom_call" | custom-call | flops 4831838208 | bytes 12582912 | tf_op jit(solution)/shard_map/spatial_filter/pallas_call | solution.py:179
  68.2 0.0 copy-start.10
  68.2 1.3 copy-done.10
  69.5 0.0 copy-start.2
  69.5 0.0 copy-start.9
  69.5 2.9 %convert.10 = bf16[3,3,256,256]{3,2,1,0:T(8,128)(2,1)} convert(f32[3,3,256,256]{3,2,1,0:T(8,128)} %get-tuple-element.9) | non-fusion elementwise | flops 589824 | bytes 3538944 | tf_op jit(solution)/shard_map/convert.5
  72.4 7.3 %all-to-all-done.1.acts = bf16[32,128,256]{2,1,0:T(8,128)(2,1)S(1)} async-done(((bf16[32,128,256]{2,1,0:T(8,128)(2,1)}), bf16[32,128,256]{2,1,0:T(8,128)(2,1)S(1)}, u32[]{:S(2)}, u32[]{:S(2)}) %all-to-all-start.1) | async-done | bytes 2097184 | tf_op jit(solution)/shard_map/all_to_all | solution.py:274
  79.7 0.0 copy-done.2
  79.7 0.0 copy-done.9
  79.7 2.6 %time_filter.1 = f32[3,256,256]{2,1,0:T(8,128)S(1)} custom-call(s32[32]{0:T(128)S(1)} %copy-done.9, bf16[32,128,256]{2,1,0:T(8,128)(2,1)S(1)} %all-to-all-done.1.acts, bf16[256,2048]{1,0:T(8,128)(2,1)S(1)} %copy-done.2), custom_call_target="tpu_custom_call" | custom-call | flops 805306368 | bytes 3145728 | tf_op jit(solution)/shard_map/time_filter/pallas_call | solution.py:261
  82.3 0.0 copy-start.12
  82.4 1.2 copy-done.12
  83.6 0.1 pad_maximum_fusion
  83.7 0.2 copy.19
  83.9 1.3 copy.17
  85.3 0.0 copy-start.6
  85.3 7.5 %all-to-all-start.2 = ((bf16[128,24,256]{2,1,0:T(8,128)(2,1)}), bf16[128,24,256]{2,1,0:T(8,128)(2,1)}, u32[]{:S(2)}, u32[]{:S(2)}) async-start(bf16[128,24,256]{2,1,0:T(8,128)(2,1)} %bitcast.16), calls=%async_computation.2 | async-start | bytes 3145728 | tf_op jit(solution)/shard_map/all_to_all | solution.py:274
  92.8 0.0 copy-done.6
  92.8 0.1 reverse_bitcast_fusion
  92.9 0.7 copy.13
  93.6 0.0 copy-start.11
  93.6 23.5 %all-to-all-done.2 = bf16[128,24,256]{2,1,0:T(8,128)(2,1)} async-done(((bf16[128,24,256]{2,1,0:T(8,128)(2,1)}), bf16[128,24,256]{2,1,0:T(8,128)(2,1)}, u32[]{:S(2)}, u32[]{:S(2)}) %all-to-all-start.2) | async-done | bytes 1572896 | tf_op jit(solution)/shard_map/all_to_all | solution.py:274
  117.1 1.7 %convert_reduce_fusion = f32[24,256]{1,0:T(8,128)S(1)} fusion(bf16[128,24,256]{2,1,0:T(8,128)(2,1)} %all-to-all-done.2), kind=kLoop, calls=%fused_computation | loop fusion | flops 1566720 | bytes 1597440 | tf_op jit(solution)/shard_map/reduce_sum | solution.py:302
  118.8 0.8 broadcast_in_dim.2
  119.6 4.6 %all-to-all-start.3 = ((bf16[32,24,256]{2,1,0:T(8,128)(2,1)}), bf16[32,24,256]{2,1,0:T(8,128)(2,1)}, u32[]{:S(2)}, u32[]{:S(2)}) async-start(bf16[32,24,256]{2,1,0:T(8,128)(2,1)} %broadcast_in_dim.2), calls=%async_computation.3 | async-start | bytes 786432 | tf_op jit(solution)/shard_map/all_to_all | solution.py:274
  124.2 0.0 copy-done.11
  124.2 8.2 %spatial_back.1 = bf16[4096,256]{1,0:T(8,128)(2,1)} custom-call(bf16[4096,256]{1,0:T(8,128)(2,1)S(1)} %copy-done.11, bf16[3,768,256]{2,1,0:T(8,128)(2,1)S(1)} %bitcast.33), custom_call_target="tpu_custom_call" | custom-call | flops 4831838208 | bytes 4194304 | tf_op jit(solution)/shard_map/spatial_back/pallas_call | solution.py:226
  132.4 2.3 %all-to-all-done.3 = bf16[32,24,256]{2,1,0:T(8,128)(2,1)} async-done(((bf16[32,24,256]{2,1,0:T(8,128)(2,1)}), bf16[32,24,256]{2,1,0:T(8,128)(2,1)}, u32[]{:S(2)}, u32[]{:S(2)}) %all-to-all-start.3) | async-done | bytes 393248 | tf_op jit(solution)/shard_map/all_to_all | solution.py:274
  134.7 1.1 convert_bitcast_fusion
  135.7 0.9 slice.8
  136.6 0.7 slice.9
  (2 shorter events, 0.0 us)
Async XLA Ops:
  0.6 1.2 copy-start
  1.9 1.0 copy-start.7
  2.9 0.7 copy-start.8
  6.7 9.7 %copy-start.3 = (bf16[1,1,64,64,256]{4,3,2,1,0:T(8,128)(2,1)S(1)}, bf16[1,1,64,64,256]{4,3,2,1,0:T(8,128)(2,1)}, u32[]{:S(2)}) copy-start(bf16[1,1,64,64,256]{4,3,2,1,0:T(8,128)(2,1)} %param.5) | copy-start | bytes 6291460
  6.7 9.7 %copy-start.5 = (bf16[3,3,256,256]{3,2,1,0:T(8,128)(2,1)S(1)}, bf16[3,3,256,256]{3,2,1,0:T(8,128)(2,1)}, u32[]{:S(2)}) copy-start(bf16[3,3,256,256]{3,2,1,0:T(8,128)(2,1)} %param.6) | copy-start | bytes 3538948
  6.7 39.9 %all-to-all-start = ((bf16[32,128,256]{2,1,0:T(8,128)(2,1)}), bf16[32,128,256]{2,1,0:T(8,128)(2,1)}, u32[]{:S(2)}, u32[]{:S(2)}) async-start(bf16[32,128,256]{2,1,0:T(8,128)(2,1)} %time_grad.1), calls=%async_computation | async-start | bytes 4194304 | tf_op jit(solution)/shard_map/all_to_all | solution.py:274
  25.3 1.4 %copy-start.4 = (bf16[4096,256]{1,0:T(8,128)(2,1)}, bf16[4096,256]{1,0:T(8,128)(2,1)S(1)}, u32[]{:S(2)}) copy-start(bf16[4096,256]{1,0:T(8,128)(2,1)S(1)} %get-tuple-element.10) | copy-start | bytes 6291460
  46.6 33.2 %all-to-all-start.1 = ((bf16[32,128,256]{2,1,0:T(8,128)(2,1)}), bf16[32,128,256]{2,1,0:T(8,128)(2,1)S(1)}, u32[]{:S(2)}, u32[]{:S(2)}) async-start(bf16[32,128,256]{2,1,0:T(8,128)(2,1)} %bitcast.31), calls=%async_computation.1 | async-start | bytes 4194304 | tf_op jit(solution)/shard_map/all_to_all | solution.py:274
  50.6 4.2 %copy-start.1 = (bf16[1,16,2,64,256]{4,3,2,1,0:T(8,128)(2,1)S(1)}, bf16[1,16,2,64,256]{4,3,2,1,0:T(8,128)(2,1)}, u32[]{:S(2)}) copy-start(bf16[1,16,2,64,256]{4,3,2,1,0:T(8,128)(2,1)} %param.8) | copy-start | bytes 3145732
  68.2 1.3 copy-start.10
  69.5 10.2 %copy-start.2 = (bf16[256,2048]{1,0:T(8,128)(2,1)S(1)}, bf16[256,2048]{1,0:T(8,128)(2,1)}, u32[]{:S(2)}) copy-start(bf16[256,2048]{1,0:T(8,128)(2,1)} %copy.18.cot_t) | copy-start | bytes 3145732
  69.5 10.2 %copy-start.9 = (s32[32]{0:T(128)S(1)}, s32[32]{0:T(128)}, u32[]{:S(2)}) copy-start(s32[32]{0:T(128)} %frame_time.3) | copy-start | bytes 388
  82.3 1.3 copy-start.12
  85.3 7.5 %copy-start.6 = (bf16[3,3,256,256]{3,2,1,0:T(8,128)(2,1)S(1)}, bf16[3,3,256,256]{3,2,1,0:T(8,128)(2,1)}, u32[]{:S(2)}) copy-start(bf16[3,3,256,256]{3,2,1,0:T(8,128)(2,1)} %param.6) | copy-start | bytes 3538948
  85.3 31.8 %all-to-all-start.2 = ((bf16[128,24,256]{2,1,0:T(8,128)(2,1)}), bf16[128,24,256]{2,1,0:T(8,128)(2,1)}, u32[]{:S(2)}, u32[]{:S(2)}) async-start(bf16[128,24,256]{2,1,0:T(8,128)(2,1)} %bitcast.16), calls=%async_computation.2 | async-start | bytes 3145728 | tf_op jit(solution)/shard_map/all_to_all | solution.py:274
  93.6 30.5 %copy-start.11 = (bf16[4096,256]{1,0:T(8,128)(2,1)S(1)}, bf16[4096,256]{1,0:T(8,128)(2,1)}, u32[]{:S(2)}) copy-start(bf16[4096,256]{1,0:T(8,128)(2,1)} %copy-done.10) | copy-start | bytes 6291460
  119.6 15.1 %all-to-all-start.3 = ((bf16[32,24,256]{2,1,0:T(8,128)(2,1)}), bf16[32,24,256]{2,1,0:T(8,128)(2,1)}, u32[]{:S(2)}, u32[]{:S(2)}) async-start(bf16[32,24,256]{2,1,0:T(8,128)(2,1)} %broadcast_in_dim.2), calls=%async_computation.3 | async-start | bytes 786432 | tf_op jit(solution)/shard_map/all_to_all | solution.py:274

commit v2 on v1

v2 whole, which is shorter than its diff:
```python
import functools
import math

import jax
import jax.numpy as jnp
from jax import lax
from jax.experimental import pallas as pl
from jax.experimental.pallas import tpu as pltpu
from jax.sharding import Mesh
from jax.sharding import PartitionSpec as P

BF16 = jnp.bfloat16
F32 = jnp.float32


def dot(a, b, dims=((1,), (0,))):
    return lax.dot_general(a, b, (dims, ((), ())), preferred_element_type=F32)


def params(mib=24):
    return pltpu.CompilerParams(vmem_limit_bytes=mib * 1024 * 1024)


def vmem():
    return pl.BlockSpec(memory_space=pltpu.VMEM)


def hbm():
    return pl.BlockSpec(memory_space=pltpu.HBM)


def smem():
    return pl.BlockSpec(memory_space=pltpu.SMEM)


def far(x):
    return pltpu.with_memory_space_constraint(x, pltpu.HBM)


def cost(flops, nbytes, trans=0):
    return pl.CostEstimate(flops=flops, bytes_accessed=nbytes, transcendentals=trans)


def spread_kernel(times, cot, out, frame_time, held, load, sent):
    half = held.shape[0]
    fetch = pltpu.make_async_copy(cot, held, load.at[0])
    order = pltpu.make_async_copy(times, frame_time, load.at[1])
    fetch.start()
    order.start()
    order.wait()
    fetch.wait()

    def send(s, carry):
        t = frame_time[s]
        pltpu.make_async_copy(held.at[t // 2], out.at[s, 0], sent).start()
        pltpu.make_async_copy(held.at[jnp.minimum((t + 1) // 2, half - 1)], out.at[s, 1], sent).start()
        return carry

    lax.fori_loop(0, out.shape[0], send, 0)
    pltpu.make_async_copy(out, out, sent).wait()


def spread_call(frame_time, cot):
    half, pixels, chans = cot.shape
    count = frame_time.shape[0]
    return pl.pallas_call(
        spread_kernel,
        out_shape=jax.ShapeDtypeStruct((count, 2, pixels, chans), BF16),
        in_specs=[hbm(), hbm()],
        out_specs=hbm(),
        scratch_shapes=[
            pltpu.SMEM((count,), jnp.int32),
            pltpu.VMEM((half, pixels, chans), BF16),
            pltpu.SemaphoreType.DMA((2,)),
            pltpu.SemaphoreType.DMA,
        ],
        compiler_params=params(60),
        cost_estimate=cost(0, 10 * half * pixels * chans),
        name="spread",
    )(frame_time, cot)


def side_by_side(block, width):
    rows, chans = block.shape
    wide = block.astype(F32)
    col = lax.rem(lax.broadcasted_iota(jnp.int32, (rows, chans), 0), width)
    left = jnp.where(col == 0, 0.0, pltpu.roll(wide, 1, 0)).astype(BF16)
    right = jnp.where(col == width - 1, 0.0, pltpu.roll(wide, rows - 1, 0)).astype(BF16)
    return left, block, right


def store_cat(cat, start, block, width):
    rows, chans = block.shape
    for j, part in enumerate(side_by_side(block, width)):
        cat[pl.ds(start, rows), j * chans : (j + 1) * chans] = part


def forward_kernel(width, x, w, acts, slope, cat):
    step = pl.program_id(0)
    pixels, chans = x.shape
    rows = acts.shape[0]

    @pl.when(step == 0)
    def _():
        cat[0:width] = jnp.zeros((width, 3 * chans), BF16)
        cat[width + pixels :] = jnp.zeros((width, 3 * chans), BF16)

        def fill(k, carry):
            at = pl.multiple_of(k * rows, rows)
            store_cat(cat, width + at, x[pl.ds(at, rows)], width)
            return carry

        lax.fori_loop(0, pixels // rows, fill, 0)

    at = pl.multiple_of(step * rows, rows)
    hidden = dot(cat[pl.ds(at, rows)], w[0])
    hidden = hidden + dot(cat[pl.ds(at + width, rows)], w[1])
    hidden = hidden + dot(cat[pl.ds(at + 2 * width, rows)], w[2])
    sig = 1.0 / (1.0 + jnp.exp(-hidden))
    acts[...] = (hidden * sig).astype(BF16)
    slope[...] = sig * (1.0 + hidden * (1.0 - sig))


def forward_call(x, w, width, steps=4):
    pixels, chans = x.shape
    rows = pixels // steps
    whole = lambda shape: pl.BlockSpec(shape, lambda k: (0,) * len(shape))
    tile = pl.BlockSpec((rows, chans), lambda k: (k, 0))
    return pl.pallas_call(
        functools.partial(forward_kernel, width),
        grid=(steps,),
        out_shape=(jax.ShapeDtypeStruct((pixels, chans), BF16), jax.ShapeDtypeStruct((pixels, chans), F32)),
        in_specs=[whole(x.shape), whole(w.shape)],
        out_specs=(tile, tile),
        scratch_shapes=[pltpu.VMEM((pixels + 2 * width, 3 * chans), BF16)],
        compiler_params=params(),
        cost_estimate=cost(18 * pixels * chans * chans, 8 * pixels * chans, 2 * pixels * chans),
        name="spatial_forward",
    )(x, w)


def filter_kernel(
    width, cuts, place, recv, slope_in, acts_in, frames_in, padded_in, w_time_in, hidden_grad, keep, send,
    w_time_t, lead, trail, slope, acts_t, frames_t, padded_t, hidden, ws, wt, arrived, left
):
    pixels, chans = slope.shape
    tile_pixels = recv.shape[2]
    edge = 2 * width

    def fetch(k):
        start, stop = cuts[k], cuts[k + 1]
        at = pl.ds(start, stop - start)
        those = pl.ds(start // tile_pixels, (stop - start) // tile_pixels)
        late = start + edge if k else 0
        beyond = pl.ds(late, stop + edge - late)
        pairs = (
            (recv.at[those, 0], lead.at[those]),
            (recv.at[those, 1], trail.at[those]),
            (slope_in.at[at], slope.at[at]),
            (acts_in.at[:, at], acts_t.at[:, at]),
            (frames_in.at[:, at], frames_t.at[:, at]),
            (padded_in.at[:, beyond], padded_t.at[:, beyond]),
        )
        return [pltpu.make_async_copy(a, b, arrived.at[k, n]) for n, (a, b) in enumerate(pairs)]

    copies = [fetch(k) for k in range(len(cuts) - 1)]
    copies[0].append(pltpu.make_async_copy(w_time_in, w_time_t, arrived.at[0, 6]))
    for copy in copies[0]:
        copy.start()

    time, core, count = place[0], place[1], place[2]
    even = lax.rem(time, 2) == 0
    has_trail = jnp.where(even, time == 0, time < count - 1)
    trail_weight = jnp.where(has_trail, 1.0, 0.0)

    def add(total, rows, at, first, term):
        rows = slice(rows * chans, (rows + 1) * chans)
        total[rows, at] = term if first else total[rows, at] + term

    leaving = []
    for k, start in enumerate(cuts[:-1]):
        stop = cuts[k + 1]
        at, those = slice(start, stop), slice(start // tile_pixels, stop // tile_pixels)
        for copy in copies[k]:
            copy.wait()
        if k == 0:
            w_lead = w_time_t[jnp.where(even, 1, 2)]
            w_trail = (w_time_t[0].astype(F32) * trail_weight).astype(BF16)
        for copy in copies[k + 1] if k + 2 < len(cuts) else ():
            copy.start()
        lead_tile = lead[those].reshape(stop - start, chans)
        trail_tile = trail[those].reshape(stop - start, chans)
        grad = (dot(lead_tile, w_lead) + dot(trail_tile, w_trail)).astype(BF16)
        block = (grad.astype(F32) * slope[at]).astype(BF16)
        hidden[at] = block
        span = pl.ds(start, stop - start)
        leaving.append(pltpu.make_async_copy(hidden.at[span], hidden_grad.at[span], left.at[k]))
        leaving[-1].start()
        add(wt, 0, slice(0, chans), k == 0, dot(acts_t[:, at], trail_tile))
        add(wt, 0, slice(chans, 2 * chans), k == 0, dot(acts_t[:, at], lead_tile))
        right = jnp.concatenate(side_by_side(block, width)[::-1], axis=1)
        above, below = padded_t[:, at], padded_t[:, start + edge : stop + edge]
        for i, rows in enumerate((above, frames_t[:, at], below)):
            add(ws, i, slice(None), k == 0, dot(rows, right))

    share = chans // 4

    def put(tap, block):
        turned = block.T
        for half in range(2):
            at = (half * 12 + tap) * share
            one = turned[2 * half * share : (2 * half + 1) * share]
            two = turned[(2 * half + 1) * share : (2 * half + 2) * share]
            keep[at : at + share] = jnp.where(core == 0, one, two)
            send[at : at + share] = jnp.where(core == 0, two, one).astype(BF16)

    for i in range(3):
        for j in range(3):
            put(3 * i + j, ws[i * chans : (i + 1) * chans, j * chans : (j + 1) * chans])
    put(9, wt[:, 0:chans] * trail_weight)
    put(10, wt[:, chans : 2 * chans] * jnp.where(even, 1.0, 0.0))
    put(11, wt[:, chans : 2 * chans] * jnp.where(even, 0.0, 1.0))
    for copy in leaving:
        copy.wait()


def filter_call(place, recv, slope, acts_t, frames_t, padded_t, w_time_t, width, pieces=(1, 1, 1, 1)):
    pixels, chans = slope.shape
    count, _, tile_pixels, _ = recv.shape
    half = (6 * chans, chans)
    cuts = [pixels * sum(pieces[:k]) // sum(pieces) for k in range(len(pieces) + 1)]
    return pl.pallas_call(
        functools.partial(filter_kernel, width, cuts),
        out_shape=(
            jax.ShapeDtypeStruct((pixels, chans), BF16),
            pltpu.VMEM(half, F32),
            pltpu.VMEM(half, BF16),
        ),
        in_specs=[smem()] + [hbm()] * 6,
        out_specs=(hbm(), vmem(), vmem()),
        scratch_shapes=[
            pltpu.VMEM(w_time_t.shape, BF16),
            pltpu.VMEM((count, tile_pixels, chans), BF16),
            pltpu.VMEM((count, tile_pixels, chans), BF16),
            pltpu.VMEM((pixels, chans), F32),
            pltpu.VMEM((chans, pixels), BF16),
            pltpu.VMEM((chans, pixels), BF16),
            pltpu.VMEM((chans, pixels + 2 * width), BF16),
            pltpu.VMEM((pixels, chans), BF16),
            pltpu.VMEM((3 * chans, 3 * chans), F32),
            pltpu.VMEM((chans, 2 * chans), F32),
            pltpu.SemaphoreType.DMA((len(pieces), 7)),
            pltpu.SemaphoreType.DMA((len(pieces),)),
        ],
        compiler_params=params(40),
        cost_estimate=cost(26 * pixels * chans * chans, 18 * pixels * chans),
        name="filters",
    )(place, *(far(x) for x in (recv, slope, acts_t, frames_t, padded_t, w_time_t)))


def back_kernel(width, hidden_grad, w, out, cat):
    step = pl.program_id(0)
    pixels, chans = hidden_grad.shape
    rows = out.shape[0]

    @pl.when(step == 0)
    def _():
        cat[0:width] = jnp.zeros((width, 3 * chans), BF16)
        cat[width + pixels :] = jnp.zeros((width, 3 * chans), BF16)

        def fill(k, carry):
            at = pl.multiple_of(k * rows, rows)
            store_cat(cat, width + at, hidden_grad[pl.ds(at, rows)], width)
            return carry

        lax.fori_loop(0, pixels // rows, fill, 0)

    at = pl.multiple_of(step * rows, rows)
    total = dot(cat[pl.ds(at, rows)], w[0])
    total = total + dot(cat[pl.ds(at + width, rows)], w[1])
    total = total + dot(cat[pl.ds(at + 2 * width, rows)], w[2])
    out[...] = total.astype(BF16)


def back_call(hidden_grad, w, width, steps=4):
    pixels, chans = hidden_grad.shape
    rows = pixels // steps
    whole = lambda shape: pl.BlockSpec(shape, lambda k: (0,) * len(shape))
    return pl.pallas_call(
        functools.partial(back_kernel, width),
        grid=(steps,),
        out_shape=jax.ShapeDtypeStruct((pixels, chans), BF16),
        in_specs=[whole(hidden_grad.shape), whole(w.shape)],
        out_specs=pl.BlockSpec((rows, chans), lambda k: (k, 0)),
        scratch_shapes=[pltpu.VMEM((pixels + 2 * width, 3 * chans), BF16)],
        compiler_params=params(),
        cost_estimate=cost(18 * pixels * chans * chans, 4 * pixels * chans),
        name="spatial_back",
    )(hidden_grad, w)


def total_kernel(factor, parts, out):
    def add(k, total):
        return total + parts[k].astype(F32)

    total = lax.fori_loop(1, parts.shape[0], add, parts[0].astype(F32), unroll=True)
    mine = (total * factor).astype(BF16)
    for k in range(out.shape[0]):
        out[k] = mine


def total_call(parts, factor, copies):
    sources, depth, chans = parts.shape
    return pl.pallas_call(
        functools.partial(total_kernel, factor),
        out_shape=jax.ShapeDtypeStruct((copies, depth, chans), BF16),
        in_specs=[vmem()],
        out_specs=vmem(),
        compiler_params=params(),
        cost_estimate=cost(sources * depth * chans, 3 * sources * depth * chans),
        name="total",
    )(parts)


def turn_kernel(rows, ws, wt):
    taps = ws.shape[0] + wt.shape[0]
    share = rows.shape[0] // taps
    for tap in range(taps):
        block = rows[tap * share : (tap + 1) * share].astype(F32)
        if tap < ws.shape[0]:
            ws[tap] = block
        else:
            wt[tap - ws.shape[0]] = block


def turn_call(rows, share):
    chans = rows.shape[1]
    return pl.pallas_call(
        turn_kernel,
        out_shape=(jax.ShapeDtypeStruct((9, share, chans), F32), jax.ShapeDtypeStruct((3, share, chans), F32)),
        in_specs=[vmem()],
        out_specs=(vmem(), vmem()),
        compiler_params=params(),
        cost_estimate=cost(0, 6 * rows.shape[0] * chans),
        name="turn",
    )(rows)


def exchange(x, axes):
    return lax.all_to_all(x, axes, split_axis=0, concat_axis=0, tiled=True)


def local(clip_frames, w_spatial, w_time, cotangent, frame_time):
    count = frame_time.shape[0]
    height, width, chans = clip_frames.shape[2:]
    pixels = height * width
    clips = lax.axis_size("clip")
    groups = lax.axis_size("half") * lax.axis_size("core")
    share = chans // groups
    x = clip_frames.reshape(pixels, chans)

    recv = exchange(spread_call(frame_time, cotangent.reshape(count // 2, -1, chans)), "clip")
    acts, slope = forward_call(x, w_spatial.reshape(3, 3 * chans, chans), width)
    padded_t = jnp.pad(x.T, ((0, 0), (width, width)))
    place = jnp.stack([frame_time[lax.axis_index("clip")], lax.axis_index("core"), jnp.int32(count)])
    hidden_grad, keep, send = filter_call(
        place, recv, slope, acts.T, x.T, padded_t, w_time.transpose(0, 2, 1), width
    )
    w_back = w_spatial[::-1, ::-1].transpose(0, 1, 3, 2).reshape(3, 3 * chans, chans)
    clip_grad = back_call(hidden_grad, w_back, width)

    came = lax.ppermute(send, "core", [(0, 1), (1, 0)])
    depth = keep.shape[0] // (2 * clips)
    parts = (keep + came.astype(F32)).astype(BF16).reshape(2 * clips, depth, chans)
    parts = exchange(parts, ("half", "clip"))
    factor = 1.0 / math.sqrt(clip_frames.shape[0] * groups * count * pixels)
    rows = exchange(total_call(parts, factor, clips), "clip")
    ws, wt = turn_call(rows.reshape(clips * depth, chans), share)
    ws = ws.reshape(3, 3, share, chans).transpose(0, 1, 3, 2)
    return (clip_grad.reshape(clip_frames.shape), ws, wt.transpose(0, 2, 1))


def solution(mesh):
    clips, groups = mesh.devices.shape
    parts = Mesh(mesh.devices.reshape(clips, 2, groups // 2), ("clip", "half", "core"))
    group = ("half", "core")
    return jax.shard_map(
        local,
        mesh=parts,
        in_specs=(
            P(group, "clip", None, None, None),
            P(),
            P(),
            P(group, None, "clip", None, None),
            P(),
        ),
        out_specs=(
            P(group, "clip", None, None, None),
            P(None, None, None, group),
            P(None, None, group),
        ),
        check_vma=False,
    )
```

time: 138 us -> 127 us (0.920)
  other arithmetic: 5.85 us -> 1.78 us
  waiting for transfers between devices: 52.9 us -> 49.3 us
  Pallas kernels: 35 us -> 32.8 us
  starting transfers between devices: 25.8 us -> 23.9 us
    all_to_all x4 -> x3, waiting for transfers between devices: 52.9 us -> 47 us  [exchange(): return lax.all_to_all(x, axes, split_axis=0, concat_axis=0, tiled=True)]
    pallas_call x0 -> x1, local copies, waits for them, and re-layouts: none -> 4.24 us  [forward_call(): pl.pallas_call(functools.partial(forward_kernel, width), grid=(steps,), o...]
    reshape x2 -> x1, local copies, waits for them, and re-layouts: 5.56 us -> 2.89 us  [local(): x = clip_frames.reshape(pixels, chans)]
    ppermute x0 -> x1, waiting for transfers between devices: none -> 2.27 us  [local(): came = lax.ppermute(send, 'core', [(0, 1), (1, 0)])]
    another operation x2 -> x1, other arithmetic: 2.97 us -> 0.71 us  [local(): jnp.stack([frame_time[lax.axis_index('clip')], lax.axis_index('core'), jn...]
    pad x0 -> x1, local copies, waits for them, and re-layouts: none -> 2.23 us  [local(): padded_t = jnp.pad(x.T, ((0, 0), (width, width)))]
    all_to_all x4 -> x3, starting transfers between devices: 25.8 us -> 23.6 us  [exchange(): return lax.all_to_all(x, axes, split_axis=0, concat_axis=0, tiled=True)]
    pallas_call x1, Pallas kernels: 8.93 us -> 7.21 us  [forward_call(): pl.pallas_call(functools.partial(forward_kernel, width), grid=(steps,), o...]
  transfers between devices with their start and end apart: 4 -> 4, of which waited for: 4 -> 4; matrix products, arithmetic and copies ran while one was open for 7% -> 11% of each run, Pallas kernels for 21% -> 12%
where the time goes in v2:
time: 127 us; the launch traced here: 126 us
  waiting for transfers between devices  49.3 us (39%)
  Pallas kernels  32.8 us (26%)
  starting transfers between devices  23.9 us (19%)
  local copies, waits for them, and re-layouts  17.6 us (14%)
  other arithmetic  1.78 us (1%)
    all_to_all x3, waiting for transfers between devices, exchange(): return lax.all_to_all(x, axes, split_axis=0, concat_axis=0, tiled=True)  47 us
    all_to_all x3, starting transfers between devices, exchange(): return lax.all_to_all(x, axes, split_axis=0, concat_axis=0, tiled=True)  23.6 us
    pallas_call x1, Pallas kernels, filter_call(): pl.pallas_call(functools.partial(filter_kernel, width, cuts), out_shape=(...  13.1 us
    pallas_call x1, Pallas kernels, back_call(): pl.pallas_call(functools.partial(back_kernel, width), grid=(steps,), out_...  7.46 us
    pallas_call x1, Pallas kernels, forward_call(): pl.pallas_call(functools.partial(forward_kernel, width), grid=(steps,), o...  7.21 us
    unnamed x17, local copies, waits for them, and re-layouts  6.81 us
    pallas_call x1, local copies, waits for them, and re-layouts, forward_call(): pl.pallas_call(functools.partial(forward_kernel, width), grid=(steps,), o...  4.24 us
    pallas_call x1, Pallas kernels, spread_call(): pl.pallas_call(spread_kernel, out_shape=jax.ShapeDtypeStruct((count, 2, p...  3.23 us
  transfers between devices with their start and end apart: 4, of which 4 were waited for; matrix products, arithmetic and copies ran while one was open for 11% of the time, Pallas kernels for 12%

profile of v2, /device:TPU:0, one launch (start us, length us, event | category | flops | bytes accessed | tf_op | source)
XLA Modules:
  0.0 126.1 jit_solution(15768021851197728405)
XLA Ops:
  0.6 3.2 %spread.1 = bf16[32,2,128,256]{3,2,1,0:T(8,128)(2,1)} custom-call(s32[32]{0:T(128)} %times.1, bf16[16,128,256]{2,1,0:T(8,128)(2,1)} %bitcast.25), custom_call_target="tpu_custom_call" | custom-call | bytes 5242880 | tf_op jit(solution)/shard_map/spread/pallas_call | solution.py:66
  3.9 0.0 copy-start.7
  3.9 0.0 copy-start
  3.9 9.5 %all-to-all-start = ((bf16[32,2,128,256]{3,2,1,0:T(8,128)(2,1)}), bf16[32,2,128,256]{3,2,1,0:T(8,128)(2,1)}, u32[]{:S(2)}, u32[]{:S(2)}) async-start(bf16[32,2,128,256]{3,2,1,0:T(8,128)(2,1)} %spread.1), calls=%async_computation | async-start | bytes 8388608 | tf_op jit(solution)/shard_map/all_to_all | solution.py:350
  13.4 0.0 copy-done.7
  13.4 0.6 dynamic_slice.3
  14.1 0.0 copy-done
  14.1 0.0 copy-start.2
  14.1 2.9 %copy.14 = bf16[4096,256]{0,1:T(8,128)(2,1)} copy(bf16[4096,256]{1,0:T(8,128)(2,1)S(1)} %bitcast.17) | data formatting | bytes 4194304 | tf_op jit(solution)/shard_map/reshape | solution.py:360
  17.0 0.0 copy-done.2
  17.0 7.2 %spatial_forward.1 = (bf16[4096,256]{1,0:T(8,128)(2,1)S(1)}, f32[4096,256]{1,0:T(8,128)S(1)}) custom-call(bf16[4096,256]{1,0:T(8,128)(2,1)S(1)} %bitcast.18, bf16[3,768,256]{2,1,0:T(8,128)(2,1)S(1)} %bitcast.20), custom_call_target="tpu_custom_call" | custom-call | flops 4831838208 | bytes 8388608 | tf_op jit(solution)/shard_map/spatial_forward/pallas_call | solution.py:129
  24.2 0.0 copy-start.1
  24.2 1.3 %copy-done.1 = bf16[4096,256]{1,0:T(8,128)(2,1)} copy-done((bf16[4096,256]{1,0:T(8,128)(2,1)}, bf16[4096,256]{1,0:T(8,128)(2,1)S(1)}, u32[]{:S(2)}) %copy-start.1) | copy-done | bytes 2097176
  25.5 0.0 copy-start.3
  25.5 2.0 %copy-done.3 = f32[4096,256]{1,0:T(8,128)} copy-done((f32[4096,256]{1,0:T(8,128)}, f32[4096,256]{1,0:T(8,128)S(1)}, u32[]{:S(2)}) %copy-start.3) | copy-done | bytes 4194328
  27.5 0.0 copy-start.6
  27.5 4.2 %copy.13 = bf16[4096,256]{0,1:T(8,128)(2,1)} copy(bf16[4096,256]{1,0:T(8,128)(2,1)} %copy-done.1) | data formatting | bytes 4194304 | tf_op jit(solution)/shard_map/spatial_forward/pallas_call | solution.py:129
  31.7 1.9 %copy.15 = bf16[3,256,256]{1,2,0:T(8,128)(2,1)} copy(bf16[3,256,256]{2,1,0:T(8,128)(2,1)} %param.7) | data formatting | bytes 786432 | tf_op args[2]
  33.6 0.0 copy-done.6
  33.6 2.2 %pad.4.padded_in = bf16[256,4224]{1,0:T(8,128)(2,1)} pad(bf16[256,4096]{1,0:T(8,128)(2,1)S(1)} %bitcast.23, bf16[]{:T(256)} %constant.17.clone.1), padding=0_0x64_64 | pad | bytes 4259842 | tf_op jit(solution)/shard_map/jit(_pad)/pad | solution.py:364
  35.9 0.7 pad_add_fusion.place
  36.6 31.0 %all-to-all-done.recv = bf16[32,2,128,256]{3,2,1,0:T(8,128)(2,1)} async-done(((bf16[32,2,128,256]{3,2,1,0:T(8,128)(2,1)}), bf16[32,2,128,256]{3,2,1,0:T(8,128)(2,1)}, u32[]{:S(2)}, u32[]{:S(2)}) %all-to-all-start) | async-done | bytes 4194336 | tf_op jit(solution)/shard_map/all_to_all | solution.py:350
  67.6 13.1 %filters.1 = (bf16[4096,256]{1,0:T(8,128)(2,1)S(1)}, f32[1536,256]{1,0:T(8,128)S(1)}, bf16[1536,256]{1,0:T(8,128)(2,1)S(1)}) custom-call(s32[3]{0:T(128)S(1)} %pad_add_fusion.place, bf16[32,2,128,256]{3,2,1,0:T(8,128)(2,1)} %all-to-all-done.recv, f32[4096,256]{1,0:T(8,128)} %copy-done.3, bf16[256,4096]{1,0:T(8,128)(2,1)} %bitcast.24, ...), custom_call_target="tpu_custom_call" | custom-call | flops 6979321856 | bytes 18874368 | tf_op jit(solution)/shard_map/filters/pallas_call | solution.py:232
  80.7 0.0 copy-start.4
  80.7 0.3 collective-permute-start
  81.0 2.3 %collective-permute-done = bf16[1536,256]{1,0:T(8,128)(2,1)S(1)} collective-permute-done((bf16[1536,256]{1,0:T(8,128)(2,1)S(1)}, bf16[1536,256]{1,0:T(8,128)(2,1)S(1)}, u32[]{:S(2)}, u32[]{:S(2)}) %collective-permute-start) | collective-permute-done | bytes 786464 | tf_op jit(solution)/shard_map/ppermute | solution.py:372
  83.2 1.1 add_convert_fusion
  84.3 0.0 copy-done.4
  84.3 10.2 %all-to-all-start.1 = ((bf16[64,24,256]{2,1,0:T(8,128)(2,1)}), bf16[64,24,256]{2,1,0:T(8,128)(2,1)S(1)}, u32[]{:S(2)}, u32[]{:S(2)}) async-start(bf16[64,24,256]{2,1,0:T(8,128)(2,1)} %bitcast.10), calls=%async_computation.1 | async-start | bytes 1572864 | tf_op jit(solution)/shard_map/all_to_all | solution.py:350
  94.5 0.1 reverse_bitcast_fusion
  94.6 0.7 copy.16
  95.3 15.0 %all-to-all-done.1.parts = bf16[64,24,256]{2,1,0:T(8,128)(2,1)S(1)} async-done(((bf16[64,24,256]{2,1,0:T(8,128)(2,1)}), bf16[64,24,256]{2,1,0:T(8,128)(2,1)S(1)}, u32[]{:S(2)}, u32[]{:S(2)}) %all-to-all-start.1) | async-done | bytes 786464 | tf_op jit(solution)/shard_map/all_to_all | solution.py:350
  110.3 0.9 total.1
  111.2 3.9 %all-to-all-start.2 = ((bf16[32,24,256]{2,1,0:T(8,128)(2,1)}), bf16[32,24,256]{2,1,0:T(8,128)(2,1)S(1)}, u32[]{:S(2)}, u32[]{:S(2)}) async-start(bf16[32,24,256]{2,1,0:T(8,128)(2,1)} %total.1), calls=%async_computation.2 | async-start | bytes 786432 | tf_op jit(solution)/shard_map/all_to_all | solution.py:350
  115.1 0.0 copy-start.5
  115.1 1.6 %copy-done.5 = bf16[4096,256]{1,0:T(8,128)(2,1)S(1)} copy-done((bf16[4096,256]{1,0:T(8,128)(2,1)S(1)}, bf16[4096,256]{1,0:T(8,128)(2,1)}, u32[]{:S(2)}) %copy-start.5) | copy-done | bytes 2097176
  116.7 7.5 %spatial_back.1 = bf16[4096,256]{1,0:T(8,128)(2,1)} custom-call(bf16[4096,256]{1,0:T(8,128)(2,1)S(1)} %copy-done.5, bf16[3,768,256]{2,1,0:T(8,128)(2,1)S(1)} %bitcast.21), custom_call_target="tpu_custom_call" | custom-call | flops 4831838208 | bytes 4194304 | tf_op jit(solution)/shard_map/spatial_back/pallas_call | solution.py:289
  124.1 1.1 all-to-all-done.2
  125.2 0.9 turn.1
Async XLA Ops:
  3.9 9.6 %copy-start.7 = (s32[32]{0:T(128)S(1)}, s32[32]{0:T(128)}, u32[]{:S(2)}) copy-start(s32[32]{0:T(128)} %times.1) | copy-start | bytes 388
  3.9 10.2 %copy-start = (bf16[1,1,64,64,256]{4,3,2,1,0:T(8,128)(2,1)S(1)}, bf16[1,1,64,64,256]{4,3,2,1,0:T(8,128)(2,1)}, u32[]{:S(2)}) copy-start(bf16[1,1,64,64,256]{4,3,2,1,0:T(8,128)(2,1)} %param.5) | copy-start | bytes 6291460
  3.9 63.7 %all-to-all-start = ((bf16[32,2,128,256]{3,2,1,0:T(8,128)(2,1)}), bf16[32,2,128,256]{3,2,1,0:T(8,128)(2,1)}, u32[]{:S(2)}, u32[]{:S(2)}) async-start(bf16[32,2,128,256]{3,2,1,0:T(8,128)(2,1)} %spread.1), calls=%async_computation | async-start | bytes 8388608 | tf_op jit(solution)/shard_map/all_to_all | solution.py:350
  14.1 2.9 %copy-start.2 = (bf16[3,3,256,256]{3,2,1,0:T(8,128)(2,1)S(1)}, bf16[3,3,256,256]{3,2,1,0:T(8,128)(2,1)}, u32[]{:S(2)}) copy-start(bf16[3,3,256,256]{3,2,1,0:T(8,128)(2,1)} %param.6) | copy-start | bytes 3538948
  24.2 1.3 %copy-start.1 = (bf16[4096,256]{1,0:T(8,128)(2,1)}, bf16[4096,256]{1,0:T(8,128)(2,1)S(1)}, u32[]{:S(2)}) copy-start(bf16[4096,256]{1,0:T(8,128)(2,1)S(1)} %get-tuple-element.11) | copy-start | bytes 6291460
  25.5 2.0 %copy-start.3 = (f32[4096,256]{1,0:T(8,128)}, f32[4096,256]{1,0:T(8,128)S(1)}, u32[]{:S(2)}) copy-start(f32[4096,256]{1,0:T(8,128)S(1)} %get-tuple-element.10.slope_in) | copy-start | bytes 12582916
  27.5 6.2 %copy-start.6 = (bf16[4096,256]{0,1:T(8,128)(2,1)S(1)}, bf16[4096,256]{0,1:T(8,128)(2,1)}, u32[]{:S(2)}) copy-start(bf16[4096,256]{0,1:T(8,128)(2,1)} %copy.14) | copy-start | bytes 6291460
  80.7 3.6 %copy-start.4 = (bf16[4096,256]{1,0:T(8,128)(2,1)}, bf16[4096,256]{1,0:T(8,128)(2,1)S(1)}, u32[]{:S(2)}) copy-start(bf16[4096,256]{1,0:T(8,128)(2,1)S(1)} %get-tuple-element.12.hidden_grad) | copy-start | bytes 6291460
  80.7 2.5 %collective-permute-start = (bf16[1536,256]{1,0:T(8,128)(2,1)S(1)}, bf16[1536,256]{1,0:T(8,128)(2,1)S(1)}, u32[]{:S(2)}, u32[]{:S(2)}) collective-permute-start(bf16[1536,256]{1,0:T(8,128)(2,1)S(1)} %get-tuple-element.14), channel_id=1, source_target_pairs={{0,1},{1,0},{2,3},{3,2},{4,5},{5,4},{6,7},{7,6},{8,9},{9,8},{10,11... | collective-permute-start | bytes 2359304 | tf_op jit(solution)/shard_map/ppermute | solution.py:372
  84.3 26.0 %all-to-all-start.1 = ((bf16[64,24,256]{2,1,0:T(8,128)(2,1)}), bf16[64,24,256]{2,1,0:T(8,128)(2,1)S(1)}, u32[]{:S(2)}, u32[]{:S(2)}) async-start(bf16[64,24,256]{2,1,0:T(8,128)(2,1)} %bitcast.10), calls=%async_computation.1 | async-start | bytes 1572864 | tf_op jit(solution)/shard_map/all_to_all | solution.py:350
  111.2 14.0 %all-to-all-start.2 = ((bf16[32,24,256]{2,1,0:T(8,128)(2,1)}), bf16[32,24,256]{2,1,0:T(8,128)(2,1)S(1)}, u32[]{:S(2)}, u32[]{:S(2)}) async-start(bf16[32,24,256]{2,1,0:T(8,128)(2,1)} %total.1), calls=%async_computation.2 | async-start | bytes 786432 | tf_op jit(solution)/shard_map/all_to_all | solution.py:350
  115.1 1.6 %copy-start.5 = (bf16[4096,256]{1,0:T(8,128)(2,1)S(1)}, bf16[4096,256]{1,0:T(8,128)(2,1)}, u32[]{:S(2)}) copy-start(bf16[4096,256]{1,0:T(8,128)(2,1)} %copy-done.4) | copy-start | bytes 6291460

commit v3 on v2

--- a/solution.py
+++ b/solution.py
@@ -373,6 +373,7 @@
     depth = keep.shape[0] // (2 * clips)
     parts = (keep + came.astype(F32)).astype(BF16).reshape(2 * clips, depth, chans)
     parts = exchange(parts, ("half", "clip"))
+    parts, clip_grad = lax.optimization_barrier((parts, clip_grad))
     factor = 1.0 / math.sqrt(clip_frames.shape[0] * groups * count * pixels)
     rows = exchange(total_call(parts, factor, clips), "clip")
     ws, wt = turn_call(rows.reshape(clips * depth, chans), share)

time: 127 us -> 126 us (level)
  blocking collectives: 0 us -> 13.8 us
  waiting for transfers between devices: 49.3 us -> 39.2 us
  starting transfers between devices: 23.9 us -> 20 us
    all_to_all x0 -> x1, blocking collectives: none -> 13.8 us  [exchange(): return lax.all_to_all(x, axes, split_axis=0, concat_axis=0, tiled=True)]
    all_to_all x3 -> x2, waiting for transfers between devices: 47 us -> 37 us  [exchange(): return lax.all_to_all(x, axes, split_axis=0, concat_axis=0, tiled=True)]
    all_to_all x3 -> x2, starting transfers between devices: 23.6 us -> 19.7 us  [exchange(): return lax.all_to_all(x, axes, split_axis=0, concat_axis=0, tiled=True)]
  transfers between devices with their start and end apart: 4 -> 3, of which waited for: 4 -> 3; matrix products, arithmetic and copies ran while one was open for 11% -> 11% of each run, Pallas kernels for 12% -> 12%
where the time goes in v3:
time: 126 us; the launch traced here: 125 us
  waiting for transfers between devices  39.2 us (31%)
  Pallas kernels  32 us (25%)
  starting transfers between devices  20 us (16%)
  local copies, waits for them, and re-layouts  17.6 us (14%)
  blocking collectives  13.8 us (11%)
  other arithmetic  1.78 us (1%)
    all_to_all x2, waiting for transfers between devices, exchange(): return lax.all_to_all(x, axes, split_axis=0, concat_axis=0, tiled=True)  37 us
    all_to_all x2, starting transfers between devices, exchange(): return lax.all_to_all(x, axes, split_axis=0, concat_axis=0, tiled=True)  19.7 us
    all_to_all x1, blocking collectives, exchange(): return lax.all_to_all(x, axes, split_axis=0, concat_axis=0, tiled=True)  13.8 us
    pallas_call x1, Pallas kernels, filter_call(): pl.pallas_call(functools.partial(filter_kernel, width, cuts), out_shape=(...  13.1 us
    pallas_call x1, Pallas kernels, back_call(): pl.pallas_call(functools.partial(back_kernel, width), grid=(steps,), out_...  7.46 us
    pallas_call x1, Pallas kernels, forward_call(): pl.pallas_call(functools.partial(forward_kernel, width), grid=(steps,), o...  7.21 us
    unnamed x17, local copies, waits for them, and re-layouts  6.8 us
    pallas_call x1, local copies, waits for them, and re-layouts, forward_call(): pl.pallas_call(functools.partial(forward_kernel, width), grid=(steps,), o...  4.26 us
  transfers between devices with their start and end apart: 3, of which 3 were waited for; matrix products, arithmetic and copies ran while one was open for 11% of the time, Pallas kernels for 12%

profile of v3, /device:TPU:0, one launch (start us, length us, event | category | flops | bytes accessed | tf_op | source)
XLA Modules:
  0.0 125.1 jit_solution(13336759369831773639)
XLA Ops:
  0.6 3.2 %spread.1 = bf16[32,2,128,256]{3,2,1,0:T(8,128)(2,1)} custom-call(s32[32]{0:T(128)} %times.1, bf16[16,128,256]{2,1,0:T(8,128)(2,1)} %bitcast.26), custom_call_target="tpu_custom_call" | custom-call | bytes 5242880 | tf_op jit(solution)/shard_map/spread/pallas_call | solution.py:66
  3.9 0.0 copy-start.7
  3.9 0.0 copy-start
  3.9 9.5 %all-to-all-start = ((bf16[32,2,128,256]{3,2,1,0:T(8,128)(2,1)}), bf16[32,2,128,256]{3,2,1,0:T(8,128)(2,1)}, u32[]{:S(2)}, u32[]{:S(2)}) async-start(bf16[32,2,128,256]{3,2,1,0:T(8,128)(2,1)} %spread.1), calls=%async_computation | async-start | bytes 8388608 | tf_op jit(solution)/shard_map/all_to_all | solution.py:350
  13.4 0.0 copy-done.7
  13.4 0.6 dynamic_slice.3
  14.0 0.0 copy-done
  14.0 0.0 copy-start.2
  14.0 2.9 %copy.14 = bf16[4096,256]{0,1:T(8,128)(2,1)} copy(bf16[4096,256]{1,0:T(8,128)(2,1)S(1)} %bitcast.17) | data formatting | bytes 4194304 | tf_op jit(solution)/shard_map/reshape | solution.py:360
  16.9 0.0 copy-done.2
  16.9 7.2 %spatial_forward.1 = (bf16[4096,256]{1,0:T(8,128)(2,1)S(1)}, f32[4096,256]{1,0:T(8,128)S(1)}) custom-call(bf16[4096,256]{1,0:T(8,128)(2,1)S(1)} %bitcast.18, bf16[3,768,256]{2,1,0:T(8,128)(2,1)S(1)} %bitcast.20), custom_call_target="tpu_custom_call" | custom-call | flops 4831838208 | bytes 8388608 | tf_op jit(solution)/shard_map/spatial_forward/pallas_call | solution.py:129
  24.1 0.0 copy-start.1
  24.1 1.3 %copy-done.1 = bf16[4096,256]{1,0:T(8,128)(2,1)} copy-done((bf16[4096,256]{1,0:T(8,128)(2,1)}, bf16[4096,256]{1,0:T(8,128)(2,1)S(1)}, u32[]{:S(2)}) %copy-start.1) | copy-done | bytes 2097176
  25.5 0.0 copy-start.3
  25.5 2.0 %copy-done.3 = f32[4096,256]{1,0:T(8,128)} copy-done((f32[4096,256]{1,0:T(8,128)}, f32[4096,256]{1,0:T(8,128)S(1)}, u32[]{:S(2)}) %copy-start.3) | copy-done | bytes 4194328
  27.4 0.0 copy-start.6
  27.4 4.3 %copy.13 = bf16[4096,256]{0,1:T(8,128)(2,1)} copy(bf16[4096,256]{1,0:T(8,128)(2,1)} %copy-done.1) | data formatting | bytes 4194304 | tf_op jit(solution)/shard_map/spatial_forward/pallas_call | solution.py:129
  31.7 1.9 %copy.15 = bf16[3,256,256]{1,2,0:T(8,128)(2,1)} copy(bf16[3,256,256]{2,1,0:T(8,128)(2,1)} %param.7) | data formatting | bytes 786432 | tf_op args[2]
  33.6 0.0 copy-done.6
  33.6 2.2 %pad.4.padded_in = bf16[256,4224]{1,0:T(8,128)(2,1)} pad(bf16[256,4096]{1,0:T(8,128)(2,1)S(1)} %bitcast.23, bf16[]{:T(256)} %constant.17.clone.1), padding=0_0x64_64 | pad | bytes 4259842 | tf_op jit(solution)/shard_map/jit(_pad)/pad | solution.py:364
  35.8 0.6 pad_add_fusion.place
  36.5 31.1 %all-to-all-done.recv = bf16[32,2,128,256]{3,2,1,0:T(8,128)(2,1)} async-done(((bf16[32,2,128,256]{3,2,1,0:T(8,128)(2,1)}), bf16[32,2,128,256]{3,2,1,0:T(8,128)(2,1)}, u32[]{:S(2)}, u32[]{:S(2)}) %all-to-all-start) | async-done | bytes 4194336 | tf_op jit(solution)/shard_map/all_to_all | solution.py:350
  67.5 13.1 %filters.1 = (bf16[4096,256]{1,0:T(8,128)(2,1)S(1)}, f32[1536,256]{1,0:T(8,128)S(1)}, bf16[1536,256]{1,0:T(8,128)(2,1)S(1)}) custom-call(s32[3]{0:T(128)S(1)} %pad_add_fusion.place, bf16[32,2,128,256]{3,2,1,0:T(8,128)(2,1)} %all-to-all-done.recv, f32[4096,256]{1,0:T(8,128)} %copy-done.3, bf16[256,4096]{1,0:T(8,128)(2,1)} %bitcast.25, ...), custom_call_target="tpu_custom_call" | custom-call | flops 6979321856 | bytes 18874368 | tf_op jit(solution)/shard_map/filters/pallas_call | solution.py:232
  80.6 0.0 copy-start.4
  80.7 0.3 collective-permute-start
  80.9 2.3 %collective-permute-done = bf16[1536,256]{1,0:T(8,128)(2,1)S(1)} collective-permute-done((bf16[1536,256]{1,0:T(8,128)(2,1)S(1)}, bf16[1536,256]{1,0:T(8,128)(2,1)S(1)}, u32[]{:S(2)}, u32[]{:S(2)}) %collective-permute-start) | collective-permute-done | bytes 786464 | tf_op jit(solution)/shard_map/ppermute | solution.py:372
  83.2 1.1 add_convert_fusion
  84.3 0.0 copy-done.4
  84.3 10.2 %all-to-all-start.1 = ((bf16[64,24,256]{2,1,0:T(8,128)(2,1)}), bf16[64,24,256]{2,1,0:T(8,128)(2,1)S(1)}, u32[]{:S(2)}, u32[]{:S(2)}) async-start(bf16[64,24,256]{2,1,0:T(8,128)(2,1)} %bitcast.24), calls=%async_computation.1 | async-start | bytes 1572864 | tf_op jit(solution)/shard_map/all_to_all | solution.py:350
  94.5 0.1 reverse_bitcast_fusion
  94.6 0.7 copy.16
  95.4 0.0 copy-start.5
  95.4 1.6 %copy-done.5 = bf16[4096,256]{1,0:T(8,128)(2,1)S(1)} copy-done((bf16[4096,256]{1,0:T(8,128)(2,1)S(1)}, bf16[4096,256]{1,0:T(8,128)(2,1)}, u32[]{:S(2)}) %copy-start.5) | copy-done | bytes 2097176
  97.0 7.5 %spatial_back.1 = bf16[4096,256]{1,0:T(8,128)(2,1)} custom-call(bf16[4096,256]{1,0:T(8,128)(2,1)S(1)} %copy-done.5, bf16[3,768,256]{2,1,0:T(8,128)(2,1)S(1)} %bitcast.21), custom_call_target="tpu_custom_call" | custom-call | flops 4831838208 | bytes 4194304 | tf_op jit(solution)/shard_map/spatial_back/pallas_call | solution.py:289
  104.4 5.9 %all-to-all-done.1.parts = bf16[64,24,256]{2,1,0:T(8,128)(2,1)S(1)} async-done(((bf16[64,24,256]{2,1,0:T(8,128)(2,1)}), bf16[64,24,256]{2,1,0:T(8,128)(2,1)S(1)}, u32[]{:S(2)}, u32[]{:S(2)}) %all-to-all-start.1) | async-done | bytes 786464 | tf_op jit(solution)/shard_map/all_to_all | solution.py:350
  110.3 0.1 total.1
  110.5 13.8 %all_to_all.15 = bf16[32,24,256]{2,1,0:T(8,128)(2,1)S(1)} all-to-all(bf16[32,24,256]{2,1,0:T(8,128)(2,1)S(1)} %total.1), channel_id=1, replica_groups=mesh['clip'=32,'half'=2,'core'=2] {'clip'}, dimensions={0} | all-to-all | bytes 786432 | tf_op jit(solution)/shard_map/all_to_all | solution.py:350
  124.2 0.9 turn.1
Async XLA Ops:
  3.9 9.6 %copy-start.7 = (s32[32]{0:T(128)S(1)}, s32[32]{0:T(128)}, u32[]{:S(2)}) copy-start(s32[32]{0:T(128)} %times.1) | copy-start | bytes 388
  3.9 10.1 %copy-start = (bf16[1,1,64,64,256]{4,3,2,1,0:T(8,128)(2,1)S(1)}, bf16[1,1,64,64,256]{4,3,2,1,0:T(8,128)(2,1)}, u32[]{:S(2)}) copy-start(bf16[1,1,64,64,256]{4,3,2,1,0:T(8,128)(2,1)} %param.5) | copy-start | bytes 6291460
  3.9 63.7 %all-to-all-start = ((bf16[32,2,128,256]{3,2,1,0:T(8,128)(2,1)}), bf16[32,2,128,256]{3,2,1,0:T(8,128)(2,1)}, u32[]{:S(2)}, u32[]{:S(2)}) async-start(bf16[32,2,128,256]{3,2,1,0:T(8,128)(2,1)} %spread.1), calls=%async_computation | async-start | bytes 8388608 | tf_op jit(solution)/shard_map/all_to_all | solution.py:350
  14.0 2.9 %copy-start.2 = (bf16[3,3,256,256]{3,2,1,0:T(8,128)(2,1)S(1)}, bf16[3,3,256,256]{3,2,1,0:T(8,128)(2,1)}, u32[]{:S(2)}) copy-start(bf16[3,3,256,256]{3,2,1,0:T(8,128)(2,1)} %param.6) | copy-start | bytes 3538948
  24.1 1.3 %copy-start.1 = (bf16[4096,256]{1,0:T(8,128)(2,1)}, bf16[4096,256]{1,0:T(8,128)(2,1)S(1)}, u32[]{:S(2)}) copy-start(bf16[4096,256]{1,0:T(8,128)(2,1)S(1)} %get-tuple-element.13) | copy-start | bytes 6291460
  25.5 2.0 %copy-start.3 = (f32[4096,256]{1,0:T(8,128)}, f32[4096,256]{1,0:T(8,128)S(1)}, u32[]{:S(2)}) copy-start(f32[4096,256]{1,0:T(8,128)S(1)} %get-tuple-element.12.slope_in) | copy-start | bytes 12582916
  27.4 6.2 %copy-start.6 = (bf16[4096,256]{0,1:T(8,128)(2,1)S(1)}, bf16[4096,256]{0,1:T(8,128)(2,1)}, u32[]{:S(2)}) copy-start(bf16[4096,256]{0,1:T(8,128)(2,1)} %copy.14) | copy-start | bytes 6291460
  80.6 3.7 %copy-start.4 = (bf16[4096,256]{1,0:T(8,128)(2,1)}, bf16[4096,256]{1,0:T(8,128)(2,1)S(1)}, u32[]{:S(2)}) copy-start(bf16[4096,256]{1,0:T(8,128)(2,1)S(1)} %get-tuple-element.16.hidden_grad) | copy-start | bytes 6291460
  80.7 2.5 %collective-permute-start = (bf16[1536,256]{1,0:T(8,128)(2,1)S(1)}, bf16[1536,256]{1,0:T(8,128)(2,1)S(1)}, u32[]{:S(2)}, u32[]{:S(2)}) collective-permute-start(bf16[1536,256]{1,0:T(8,128)(2,1)S(1)} %get-tuple-element.15), channel_id=1, source_target_pairs={{0,1},{1,0},{2,3},{3,2},{4,5},{5,4},{6,7},{7,6},{8,9},{9,8},{10,11... | collective-permute-start | bytes 2359304 | tf_op jit(solution)/shard_map/ppermute | solution.py:372
  84.3 26.0 %all-to-all-start.1 = ((bf16[64,24,256]{2,1,0:T(8,128)(2,1)}), bf16[64,24,256]{2,1,0:T(8,128)(2,1)S(1)}, u32[]{:S(2)}, u32[]{:S(2)}) async-start(bf16[64,24,256]{2,1,0:T(8,128)(2,1)} %bitcast.24), calls=%async_computation.1 | async-start | bytes 1572864 | tf_op jit(solution)/shard_map/all_to_all | solution.py:350
  95.4 1.6 %copy-start.5 = (bf16[4096,256]{1,0:T(8,128)(2,1)S(1)}, bf16[4096,256]{1,0:T(8,128)(2,1)}, u32[]{:S(2)}) copy-start(bf16[4096,256]{1,0:T(8,128)(2,1)} %copy-done.4) | copy-start | bytes 6291460

commit v4 on v3

--- a/solution.py
+++ b/solution.py
@@ -9,6 +9,7 @@
 from jax.sharding import Mesh
 from jax.sharding import PartitionSpec as P
 
+SPREAD = 4
 BF16 = jnp.bfloat16
 F32 = jnp.float32
 
@@ -41,22 +42,32 @@
     return pl.CostEstimate(flops=flops, bytes_accessed=nbytes, transcendentals=trans)
 
 
-def spread_kernel(times, cot, out, frame_time, held, load, sent):
+def spread_kernel(times, cot, out, frame_time, place, held, load, sent):
     half = held.shape[0]
-    fetch = pltpu.make_async_copy(cot, held, load.at[0])
-    order = pltpu.make_async_copy(times, frame_time, load.at[1])
-    fetch.start()
+    count = out.shape[0]
+    order = pltpu.make_async_copy(times, frame_time, load.at[0])
     order.start()
+    span = half // (load.shape[0] - 1)
+    pieces = []
+    for k in range(load.shape[0] - 1):
+        at = pl.ds(k * span, span)
+        pieces.append(pltpu.make_async_copy(cot.at[at], held.at[at], load.at[k + 1]))
+        pieces[-1].start()
     order.wait()
-    fetch.wait()
-
-    def send(s, carry):
-        t = frame_time[s]
-        pltpu.make_async_copy(held.at[t // 2], out.at[s, 0], sent).start()
-        pltpu.make_async_copy(held.at[jnp.minimum((t + 1) // 2, half - 1)], out.at[s, 1], sent).start()
+
+    def put(s, carry):
+        place[frame_time[s]] = s
         return carry
 
-    lax.fori_loop(0, out.shape[0], send, 0)
+    lax.fori_loop(0, count, put, 0)
+    for k, piece in enumerate(pieces):
+        piece.wait()
+        for u in range(k * span, (k + 1) * span):
+            leads = (2 * u, 2 * u + 1)
+            trails = tuple(t for t in range(count) if min((t + 1) // 2, half - 1) == u)
+            for which, wanted in enumerate((leads, trails)):
+                for t in wanted:
+                    pltpu.make_async_copy(held.at[u], out.at[place[t], which], sent).start()
     pltpu.make_async_copy(out, out, sent).wait()
 
 
@@ -70,8 +81,9 @@
         out_specs=hbm(),
         scratch_shapes=[
             pltpu.SMEM((count,), jnp.int32),
+            pltpu.SMEM((count,), jnp.int32),
             pltpu.VMEM((half, pixels, chans), BF16),
-            pltpu.SemaphoreType.DMA((2,)),
+            pltpu.SemaphoreType.DMA((SPREAD + 1,)),
             pltpu.SemaphoreType.DMA,
         ],
         compiler_params=params(60),
@@ -83,7 +95,7 @@
 def side_by_side(block, width):
     rows, chans = block.shape
     wide = block.astype(F32)
-    col = lax.rem(lax.broadcasted_iota(jnp.int32, (rows, chans), 0), width)
+    col = lax.broadcasted_iota(jnp.int32, (rows, chans), 0) & (width - 1)
     left = jnp.where(col == 0, 0.0, pltpu.roll(wide, 1, 0)).astype(BF16)
     right = jnp.where(col == width - 1, 0.0, pltpu.roll(wide, rows - 1, 0)).astype(BF16)
     return left, block, right
@@ -173,9 +185,23 @@
     has_trail = jnp.where(even, time == 0, time < count - 1)
     trail_weight = jnp.where(has_trail, 1.0, 0.0)
 
-    def add(total, rows, at, first, term):
+    share = chans // 4
+
+    def put(tap, block):
+        turned = block.T
+        for half in range(2):
+            at = (half * 12 + tap) * share
+            one = turned[2 * half * share : (2 * half + 1) * share]
+            two = turned[(2 * half + 1) * share : (2 * half + 2) * share]
+            keep[at : at + share] = jnp.where(core == 0, one, two)
+            send[at : at + share] = jnp.where(core == 0, two, one).astype(BF16)
+
+    def add(total, rows, at, k, term):
         rows = slice(rows * chans, (rows + 1) * chans)
-        total[rows, at] = term if first else total[rows, at] + term
+        term = total[rows, at] + term if k else term
+        if k + 2 < len(cuts):
+            total[rows, at] = term
+        return term
 
     leaving = []
     for k, start in enumerate(cuts[:-1]):
@@ -196,30 +222,19 @@
         span = pl.ds(start, stop - start)
         leaving.append(pltpu.make_async_copy(hidden.at[span], hidden_grad.at[span], left.at[k]))
         leaving[-1].start()
-        add(wt, 0, slice(0, chans), k == 0, dot(acts_t[:, at], trail_tile))
-        add(wt, 0, slice(chans, 2 * chans), k == 0, dot(acts_t[:, at], lead_tile))
+        last = k + 2 == len(cuts)
+        trail_term = add(wt, 0, slice(0, chans), k, dot(acts_t[:, at], trail_tile))
+        lead_term = add(wt, 0, slice(chans, 2 * chans), k, dot(acts_t[:, at], lead_tile))
         right = jnp.concatenate(side_by_side(block, width)[::-1], axis=1)
         above, below = padded_t[:, at], padded_t[:, start + edge : stop + edge]
+        if last:
+            put(9, trail_term * trail_weight)
+            put(10, lead_term * jnp.where(even, 1.0, 0.0))
+            put(11, lead_term * jnp.where(even, 0.0, 1.0))
         for i, rows in enumerate((above, frames_t[:, at], below)):
-            add(ws, i, slice(None), k == 0, dot(rows, right))
-
-    share = chans // 4
-
-    def put(tap, block):
-        turned = block.T
-        for half in range(2):
-            at = (half * 12 + tap) * share
-            one = turned[2 * half * share : (2 * half + 1) * share]
-            two = turned[(2 * half + 1) * share : (2 * half + 2) * share]
-            keep[at : at + share] = jnp.where(core == 0, one, two)
-            send[at : at + share] = jnp.where(core == 0, two, one).astype(BF16)
-
-    for i in range(3):
-        for j in range(3):
-            put(3 * i + j, ws[i * chans : (i + 1) * chans, j * chans : (j + 1) * chans])
-    put(9, wt[:, 0:chans] * trail_weight)
-    put(10, wt[:, chans : 2 * chans] * jnp.where(even, 1.0, 0.0))
-    put(11, wt[:, chans : 2 * chans] * jnp.where(even, 0.0, 1.0))
+            term = add(ws, i, slice(None), k, dot(rows, right))
+            for j in range(3) if last else ():
+                put(3 * i + j, term[:, j * chans : (j + 1) * chans])
     for copy in leaving:
         copy.wait()
 
@@ -232,7 +247,7 @@
     return pl.pallas_call(
         functools.partial(filter_kernel, width, cuts),
         out_shape=(
-            jax.ShapeDtypeStruct((pixels, chans), BF16),
+            pltpu.HBM((pixels, chans), BF16),
             pltpu.VMEM(half, F32),
             pltpu.VMEM(half, BF16),
         ),

time: 126 us -> 124 us (0.984)
  Pallas kernels: 32 us -> 30.5 us
    pallas_call x1, Pallas kernels: 13.1 us -> 11.7 us  [filter_call(): pl.pallas_call(functools.partial(filter_kernel, width, cuts), out_shape=(...]
    unnamed x17 -> x15, local copies, waits for them, and re-layouts: 6.8 us -> 6.8 us
where the time goes in v4:
time: 124 us; the launch traced here: 123 us
  waiting for transfers between devices  38.9 us (31%)
  Pallas kernels  30.5 us (25%)
  starting transfers between devices  19.8 us (16%)
  local copies, waits for them, and re-layouts  17.8 us (14%)
  blocking collectives  13.8 us (11%)
  other arithmetic  1.9 us (2%)
    all_to_all x2, waiting for transfers between devices, exchange(): return lax.all_to_all(x, axes, split_axis=0, concat_axis=0, tiled=True)  36.7 us
    all_to_all x2, starting transfers between devices, exchange(): return lax.all_to_all(x, axes, split_axis=0, concat_axis=0, tiled=True)  19.7 us
    all_to_all x1, blocking collectives, exchange(): return lax.all_to_all(x, axes, split_axis=0, concat_axis=0, tiled=True)  13.8 us
    pallas_call x1, Pallas kernels, filter_call(): pl.pallas_call(functools.partial(filter_kernel, width, cuts), out_shape=(...  11.7 us
    pallas_call x1, Pallas kernels, back_call(): pl.pallas_call(functools.partial(back_kernel, width), grid=(steps,), out_...  7.46 us
    pallas_call x1, Pallas kernels, forward_call(): pl.pallas_call(functools.partial(forward_kernel, width), grid=(steps,), o...  7.21 us
    unnamed x15, local copies, waits for them, and re-layouts  6.8 us
    pallas_call x1, local copies, waits for them, and re-layouts, forward_call(): pl.pallas_call(functools.partial(forward_kernel, width), grid=(steps,), o...  4.27 us
  transfers between devices with their start and end apart: 3, of which 3 were waited for; matrix products, arithmetic and copies ran while one was open for 11% of the time, Pallas kernels for 12%

profile of v4, /device:TPU:0, one launch (start us, length us, event | category | flops | bytes accessed | tf_op | source)
XLA Modules:
  0.0 123.4 jit_solution(6237687644916836161)
XLA Ops:
  0.6 3.0 %spread.1 = bf16[32,2,128,256]{3,2,1,0:T(8,128)(2,1)} custom-call(s32[32]{0:T(128)} %times.1, bf16[16,128,256]{2,1,0:T(8,128)(2,1)} %bitcast.26), custom_call_target="tpu_custom_call" | custom-call | bytes 5242880 | tf_op jit(solution)/shard_map/spread/pallas_call | solution.py:77
  3.7 0.0 copy-start.6
  3.7 0.0 copy-start
  3.7 9.5 %all-to-all-start = ((bf16[32,2,128,256]{3,2,1,0:T(8,128)(2,1)}), bf16[32,2,128,256]{3,2,1,0:T(8,128)(2,1)}, u32[]{:S(2)}, u32[]{:S(2)}) async-start(bf16[32,2,128,256]{3,2,1,0:T(8,128)(2,1)} %spread.1), calls=%async_computation | async-start | bytes 8388608 | tf_op jit(solution)/shard_map/all_to_all | solution.py:365
  13.2 0.0 copy-done.6
  13.2 0.7 dynamic_slice.3
  13.9 0.0 copy-done
  13.9 0.0 copy-start.2
  13.9 3.0 %copy.14 = bf16[4096,256]{0,1:T(8,128)(2,1)} copy(bf16[4096,256]{1,0:T(8,128)(2,1)S(1)} %bitcast.17) | data formatting | bytes 4194304 | tf_op jit(solution)/shard_map/reshape | solution.py:375
  16.9 0.0 copy-done.2
  16.9 7.2 %spatial_forward.1 = (bf16[4096,256]{1,0:T(8,128)(2,1)S(1)}, f32[4096,256]{1,0:T(8,128)S(1)}) custom-call(bf16[4096,256]{1,0:T(8,128)(2,1)S(1)} %bitcast.18, bf16[3,768,256]{2,1,0:T(8,128)(2,1)S(1)} %bitcast.20), custom_call_target="tpu_custom_call" | custom-call | flops 4831838208 | bytes 8388608 | tf_op jit(solution)/shard_map/spatial_forward/pallas_call | solution.py:141
  24.1 0.0 copy-start.1
  24.1 1.3 %copy-done.1 = bf16[4096,256]{1,0:T(8,128)(2,1)} copy-done((bf16[4096,256]{1,0:T(8,128)(2,1)}, bf16[4096,256]{1,0:T(8,128)(2,1)S(1)}, u32[]{:S(2)}) %copy-start.1) | copy-done | bytes 2097176
  25.4 0.0 copy-start.3
  25.4 2.0 %copy-done.3 = f32[4096,256]{1,0:T(8,128)} copy-done((f32[4096,256]{1,0:T(8,128)}, f32[4096,256]{1,0:T(8,128)S(1)}, u32[]{:S(2)}) %copy-start.3) | copy-done | bytes 4194328
  27.4 0.0 copy-start.5
  27.4 4.3 %copy.13 = bf16[4096,256]{0,1:T(8,128)(2,1)} copy(bf16[4096,256]{1,0:T(8,128)(2,1)} %copy-done.1) | data formatting | bytes 4194304 | tf_op jit(solution)/shard_map/spatial_forward/pallas_call | solution.py:141
  31.7 1.9 %copy.15 = bf16[3,256,256]{1,2,0:T(8,128)(2,1)} copy(bf16[3,256,256]{2,1,0:T(8,128)(2,1)} %param.7) | data formatting | bytes 786432 | tf_op args[2]
  33.6 0.0 copy-done.5
  33.6 2.2 %pad.4.padded_in = bf16[256,4224]{1,0:T(8,128)(2,1)} pad(bf16[256,4096]{1,0:T(8,128)(2,1)S(1)} %bitcast.23, bf16[]{:T(256)} %constant.17.clone.1), padding=0_0x64_64 | pad | bytes 4259842 | tf_op jit(solution)/shard_map/jit(_pad)/pad | solution.py:379
  35.8 0.8 pad_add_fusion.place
  36.6 30.8 %all-to-all-done.recv = bf16[32,2,128,256]{3,2,1,0:T(8,128)(2,1)} async-done(((bf16[32,2,128,256]{3,2,1,0:T(8,128)(2,1)}), bf16[32,2,128,256]{3,2,1,0:T(8,128)(2,1)}, u32[]{:S(2)}, u32[]{:S(2)}) %all-to-all-start) | async-done | bytes 4194336 | tf_op jit(solution)/shard_map/all_to_all | solution.py:365
  67.3 11.7 %filters.1 = (bf16[4096,256]{1,0:T(8,128)(2,1)}, f32[1536,256]{1,0:T(8,128)S(1)}, bf16[1536,256]{1,0:T(8,128)(2,1)S(1)}) custom-call(s32[3]{0:T(128)S(1)} %pad_add_fusion.place, bf16[32,2,128,256]{3,2,1,0:T(8,128)(2,1)} %all-to-all-done.recv, f32[4096,256]{1,0:T(8,128)} %copy-done.3, bf16[256,4096]{1,0:T(8,128)(2,1)} %bitcast.25, ...), custom_call_target="tpu_custom_call" | custom-call | flops 6979321856 | bytes 18874368 | tf_op jit(solution)/shard_map/filters/pallas_call | solution.py:247
  79.1 0.1 collective-permute-start
  79.2 2.3 %collective-permute-done = bf16[1536,256]{1,0:T(8,128)(2,1)S(1)} collective-permute-done((bf16[1536,256]{1,0:T(8,128)(2,1)S(1)}, bf16[1536,256]{1,0:T(8,128)(2,1)S(1)}, u32[]{:S(2)}, u32[]{:S(2)}) %collective-permute-start) | collective-permute-done | bytes 786464 | tf_op jit(solution)/shard_map/ppermute | solution.py:387
  81.4 1.1 add_convert_fusion
  82.6 10.2 %all-to-all-start.1 = ((bf16[64,24,256]{2,1,0:T(8,128)(2,1)}), bf16[64,24,256]{2,1,0:T(8,128)(2,1)S(1)}, u32[]{:S(2)}, u32[]{:S(2)}) async-start(bf16[64,24,256]{2,1,0:T(8,128)(2,1)} %bitcast.24), calls=%async_computation.1 | async-start | bytes 1572864 | tf_op jit(solution)/shard_map/all_to_all | solution.py:365
  92.8 0.1 reverse_bitcast_fusion
  92.8 0.7 copy.16
  93.6 0.0 copy-start.4
  93.6 1.6 %copy-done.4 = bf16[4096,256]{1,0:T(8,128)(2,1)S(1)} copy-done((bf16[4096,256]{1,0:T(8,128)(2,1)S(1)}, bf16[4096,256]{1,0:T(8,128)(2,1)}, u32[]{:S(2)}) %copy-start.4) | copy-done | bytes 2097176
  95.2 7.5 %spatial_back.1 = bf16[4096,256]{1,0:T(8,128)(2,1)} custom-call(bf16[4096,256]{1,0:T(8,128)(2,1)S(1)} %copy-done.4, bf16[3,768,256]{2,1,0:T(8,128)(2,1)S(1)} %bitcast.21), custom_call_target="tpu_custom_call" | custom-call | flops 4831838208 | bytes 4194304 | tf_op jit(solution)/shard_map/spatial_back/pallas_call | solution.py:304
  102.6 5.9 %all-to-all-done.1.parts = bf16[64,24,256]{2,1,0:T(8,128)(2,1)S(1)} async-done(((bf16[64,24,256]{2,1,0:T(8,128)(2,1)}), bf16[64,24,256]{2,1,0:T(8,128)(2,1)S(1)}, u32[]{:S(2)}, u32[]{:S(2)}) %all-to-all-start.1) | async-done | bytes 786464 | tf_op jit(solution)/shard_map/all_to_all | solution.py:365
  108.5 0.1 total.1
  108.7 13.8 %all_to_all.15 = bf16[32,24,256]{2,1,0:T(8,128)(2,1)S(1)} all-to-all(bf16[32,24,256]{2,1,0:T(8,128)(2,1)S(1)} %total.1), channel_id=1, replica_groups=mesh['clip'=32,'half'=2,'core'=2] {'clip'}, dimensions={0} | all-to-all | bytes 786432 | tf_op jit(solution)/shard_map/all_to_all | solution.py:365
  122.5 0.9 turn.1
Async XLA Ops:
  3.7 9.6 %copy-start.6 = (s32[32]{0:T(128)S(1)}, s32[32]{0:T(128)}, u32[]{:S(2)}) copy-start(s32[32]{0:T(128)} %times.1) | copy-start | bytes 388
  3.7 10.2 %copy-start = (bf16[1,1,64,64,256]{4,3,2,1,0:T(8,128)(2,1)S(1)}, bf16[1,1,64,64,256]{4,3,2,1,0:T(8,128)(2,1)}, u32[]{:S(2)}) copy-start(bf16[1,1,64,64,256]{4,3,2,1,0:T(8,128)(2,1)} %param.5) | copy-start | bytes 6291460
  3.7 63.7 %all-to-all-start = ((bf16[32,2,128,256]{3,2,1,0:T(8,128)(2,1)}), bf16[32,2,128,256]{3,2,1,0:T(8,128)(2,1)}, u32[]{:S(2)}, u32[]{:S(2)}) async-start(bf16[32,2,128,256]{3,2,1,0:T(8,128)(2,1)} %spread.1), calls=%async_computation | async-start | bytes 8388608 | tf_op jit(solution)/shard_map/all_to_all | solution.py:365
  13.9 3.0 %copy-start.2 = (bf16[3,3,256,256]{3,2,1,0:T(8,128)(2,1)S(1)}, bf16[3,3,256,256]{3,2,1,0:T(8,128)(2,1)}, u32[]{:S(2)}) copy-start(bf16[3,3,256,256]{3,2,1,0:T(8,128)(2,1)} %param.6) | copy-start | bytes 3538948
  24.1 1.3 %copy-start.1 = (bf16[4096,256]{1,0:T(8,128)(2,1)}, bf16[4096,256]{1,0:T(8,128)(2,1)S(1)}, u32[]{:S(2)}) copy-start(bf16[4096,256]{1,0:T(8,128)(2,1)S(1)} %get-tuple-element.13) | copy-start | bytes 6291460
  25.4 2.0 %copy-start.3 = (f32[4096,256]{1,0:T(8,128)}, f32[4096,256]{1,0:T(8,128)S(1)}, u32[]{:S(2)}) copy-start(f32[4096,256]{1,0:T(8,128)S(1)} %get-tuple-element.12.slope_in) | copy-start | bytes 12582916
  27.4 6.2 %copy-start.5 = (bf16[4096,256]{0,1:T(8,128)(2,1)S(1)}, bf16[4096,256]{0,1:T(8,128)(2,1)}, u32[]{:S(2)}) copy-start(bf16[4096,256]{0,1:T(8,128)(2,1)} %copy.14) | copy-start | bytes 6291460
  79.1 2.4 %collective-permute-start = (bf16[1536,256]{1,0:T(8,128)(2,1)S(1)}, bf16[1536,256]{1,0:T(8,128)(2,1)S(1)}, u32[]{:S(2)}, u32[]{:S(2)}) collective-permute-start(bf16[1536,256]{1,0:T(8,128)(2,1)S(1)} %get-tuple-element.15), channel_id=1, source_target_pairs={{0,1},{1,0},{2,3},{3,2},{4,5},{5,4},{6,7},{7,6},{8,9},{9,8},{10,11... | collective-permute-start | bytes 2359304 | tf_op jit(solution)/shard_map/ppermute | solution.py:387
  82.6 26.0 %all-to-all-start.1 = ((bf16[64,24,256]{2,1,0:T(8,128)(2,1)}), bf16[64,24,256]{2,1,0:T(8,128)(2,1)S(1)}, u32[]{:S(2)}, u32[]{:S(2)}) async-start(bf16[64,24,256]{2,1,0:T(8,128)(2,1)} %bitcast.24), calls=%async_computation.1 | async-start | bytes 1572864 | tf_op jit(solution)/shard_map/all_to_all | solution.py:365
  93.6 1.6 %copy-start.4 = (bf16[4096,256]{1,0:T(8,128)(2,1)S(1)}, bf16[4096,256]{1,0:T(8,128)(2,1)}, u32[]{:S(2)}) copy-start(bf16[4096,256]{1,0:T(8,128)(2,1)} %get-tuple-element.16.hidden_grad) | copy-start | bytes 6291460

commit v5 on v4

--- a/solution.py
+++ b/solution.py
@@ -214,6 +214,8 @@
             w_trail = (w_time_t[0].astype(F32) * trail_weight).astype(BF16)
         for copy in copies[k + 1] if k + 2 < len(cuts) else ():
             copy.start()
+        for copy in leaving[-1:]:
+            copy.start()
         lead_tile = lead[those].reshape(stop - start, chans)
         trail_tile = trail[those].reshape(stop - start, chans)
         grad = (dot(lead_tile, w_lead) + dot(trail_tile, w_trail)).astype(BF16)
@@ -221,7 +223,6 @@
         hidden[at] = block
         span = pl.ds(start, stop - start)
         leaving.append(pltpu.make_async_copy(hidden.at[span], hidden_grad.at[span], left.at[k]))
-        leaving[-1].start()
         last = k + 2 == len(cuts)
         trail_term = add(wt, 0, slice(0, chans), k, dot(acts_t[:, at], trail_tile))
         lead_term = add(wt, 0, slice(chans, 2 * chans), k, dot(acts_t[:, at], lead_tile))
@@ -235,6 +236,7 @@
             term = add(ws, i, slice(None), k, dot(rows, right))
             for j in range(3) if last else ():
                 put(3 * i + j, term[:, j * chans : (j + 1) * chans])
+    leaving[-1].start()
     for copy in leaving:
         copy.wait()
 

time: 124 us -> 124 us (level)
  no operation moved by 1% of the time
where the time goes in v5:
time: 124 us; the launch traced here: 123 us
  waiting for transfers between devices  38.9 us (31%)
  Pallas kernels  30.3 us (24%)
  starting transfers between devices  19.8 us (16%)
  local copies, waits for them, and re-layouts  17.8 us (14%)
  blocking collectives  13.8 us (11%)
  other arithmetic  1.9 us (2%)
    all_to_all x2, waiting for transfers between devices, exchange(): return lax.all_to_all(x, axes, split_axis=0, concat_axis=0, tiled=True)  36.7 us
    all_to_all x2, starting transfers between devices, exchange(): return lax.all_to_all(x, axes, split_axis=0, concat_axis=0, tiled=True)  19.7 us
    all_to_all x1, blocking collectives, exchange(): return lax.all_to_all(x, axes, split_axis=0, concat_axis=0, tiled=True)  13.8 us
    pallas_call x1, Pallas kernels, filter_call(): pl.pallas_call(functools.partial(filter_kernel, width, cuts), out_shape=(...  11.5 us
    pallas_call x1, Pallas kernels, back_call(): pl.pallas_call(functools.partial(back_kernel, width), grid=(steps,), out_...  7.46 us
    pallas_call x1, Pallas kernels, forward_call(): pl.pallas_call(functools.partial(forward_kernel, width), grid=(steps,), o...  7.21 us
    unnamed x15, local copies, waits for them, and re-layouts  6.8 us
    pallas_call x1, local copies, waits for them, and re-layouts, forward_call(): pl.pallas_call(functools.partial(forward_kernel, width), grid=(steps,), o...  4.27 us
  transfers between devices with their start and end apart: 3, of which 3 were waited for; matrix products, arithmetic and copies ran while one was open for 11% of the time, Pallas kernels for 12%

profile of v5, /device:TPU:0, one launch (start us, length us, event | category | flops | bytes accessed | tf_op | source)
XLA Modules:
  0.0 123.3 jit_solution(2544115313359521493)
XLA Ops:
  0.6 3.1 %spread.1 = bf16[32,2,128,256]{3,2,1,0:T(8,128)(2,1)} custom-call(s32[32]{0:T(128)} %times.1, bf16[16,128,256]{2,1,0:T(8,128)(2,1)} %bitcast.26), custom_call_target="tpu_custom_call" | custom-call | bytes 5242880 | tf_op jit(solution)/shard_map/spread/pallas_call | solution.py:77
  3.7 0.0 copy-start.6
  3.7 0.0 copy-start
  3.7 9.5 %all-to-all-start = ((bf16[32,2,128,256]{3,2,1,0:T(8,128)(2,1)}), bf16[32,2,128,256]{3,2,1,0:T(8,128)(2,1)}, u32[]{:S(2)}, u32[]{:S(2)}) async-start(bf16[32,2,128,256]{3,2,1,0:T(8,128)(2,1)} %spread.1), calls=%async_computation | async-start | bytes 8388608 | tf_op jit(solution)/shard_map/all_to_all | solution.py:367
  13.3 0.0 copy-done.6
  13.3 0.7 dynamic_slice.3
  14.0 0.0 copy-done
  14.0 0.0 copy-start.2
  14.0 3.0 %copy.14 = bf16[4096,256]{0,1:T(8,128)(2,1)} copy(bf16[4096,256]{1,0:T(8,128)(2,1)S(1)} %bitcast.17) | data formatting | bytes 4194304 | tf_op jit(solution)/shard_map/reshape | solution.py:377
  17.0 0.0 copy-done.2
  17.0 7.2 %spatial_forward.1 = (bf16[4096,256]{1,0:T(8,128)(2,1)S(1)}, f32[4096,256]{1,0:T(8,128)S(1)}) custom-call(bf16[4096,256]{1,0:T(8,128)(2,1)S(1)} %bitcast.18, bf16[3,768,256]{2,1,0:T(8,128)(2,1)S(1)} %bitcast.20), custom_call_target="tpu_custom_call" | custom-call | flops 4831838208 | bytes 8388608 | tf_op jit(solution)/shard_map/spatial_forward/pallas_call | solution.py:141
  24.2 0.0 copy-start.1
  24.2 1.3 %copy-done.1 = bf16[4096,256]{1,0:T(8,128)(2,1)} copy-done((bf16[4096,256]{1,0:T(8,128)(2,1)}, bf16[4096,256]{1,0:T(8,128)(2,1)S(1)}, u32[]{:S(2)}) %copy-start.1) | copy-done | bytes 2097176
  25.5 0.0 copy-start.3
  25.5 2.0 %copy-done.3 = f32[4096,256]{1,0:T(8,128)} copy-done((f32[4096,256]{1,0:T(8,128)}, f32[4096,256]{1,0:T(8,128)S(1)}, u32[]{:S(2)}) %copy-start.3) | copy-done | bytes 4194328
  27.5 0.0 copy-start.5
  27.5 4.3 %copy.13 = bf16[4096,256]{0,1:T(8,128)(2,1)} copy(bf16[4096,256]{1,0:T(8,128)(2,1)} %copy-done.1) | data formatting | bytes 4194304 | tf_op jit(solution)/shard_map/spatial_forward/pallas_call | solution.py:141
  31.7 1.9 %copy.15 = bf16[3,256,256]{1,2,0:T(8,128)(2,1)} copy(bf16[3,256,256]{2,1,0:T(8,128)(2,1)} %param.7) | data formatting | bytes 786432 | tf_op args[2]
  33.7 0.0 copy-done.5
  33.7 2.2 %pad.4.padded_in = bf16[256,4224]{1,0:T(8,128)(2,1)} pad(bf16[256,4096]{1,0:T(8,128)(2,1)S(1)} %bitcast.23, bf16[]{:T(256)} %constant.17.clone.1), padding=0_0x64_64 | pad | bytes 4259842 | tf_op jit(solution)/shard_map/jit(_pad)/pad | solution.py:381
  35.9 0.8 pad_add_fusion.place
  36.6 30.8 %all-to-all-done.recv = bf16[32,2,128,256]{3,2,1,0:T(8,128)(2,1)} async-done(((bf16[32,2,128,256]{3,2,1,0:T(8,128)(2,1)}), bf16[32,2,128,256]{3,2,1,0:T(8,128)(2,1)}, u32[]{:S(2)}, u32[]{:S(2)}) %all-to-all-start) | async-done | bytes 4194336 | tf_op jit(solution)/shard_map/all_to_all | solution.py:367
  67.4 11.5 %filters.1 = (bf16[4096,256]{1,0:T(8,128)(2,1)}, f32[1536,256]{1,0:T(8,128)S(1)}, bf16[1536,256]{1,0:T(8,128)(2,1)S(1)}) custom-call(s32[3]{0:T(128)S(1)} %pad_add_fusion.place, bf16[32,2,128,256]{3,2,1,0:T(8,128)(2,1)} %all-to-all-done.recv, f32[4096,256]{1,0:T(8,128)} %copy-done.3, bf16[256,4096]{1,0:T(8,128)(2,1)} %bitcast.25, ...), custom_call_target="tpu_custom_call" | custom-call | flops 6979321856 | bytes 18874368 | tf_op jit(solution)/shard_map/filters/pallas_call | solution.py:249
  78.9 0.1 collective-permute-start
  79.0 2.3 %collective-permute-done = bf16[1536,256]{1,0:T(8,128)(2,1)S(1)} collective-permute-done((bf16[1536,256]{1,0:T(8,128)(2,1)S(1)}, bf16[1536,256]{1,0:T(8,128)(2,1)S(1)}, u32[]{:S(2)}, u32[]{:S(2)}) %collective-permute-start) | collective-permute-done | bytes 786464 | tf_op jit(solution)/shard_map/ppermute | solution.py:389
  81.3 1.1 add_convert_fusion
  82.5 10.2 %all-to-all-start.1 = ((bf16[64,24,256]{2,1,0:T(8,128)(2,1)}), bf16[64,24,256]{2,1,0:T(8,128)(2,1)S(1)}, u32[]{:S(2)}, u32[]{:S(2)}) async-start(bf16[64,24,256]{2,1,0:T(8,128)(2,1)} %bitcast.24), calls=%async_computation.1 | async-start | bytes 1572864 | tf_op jit(solution)/shard_map/all_to_all | solution.py:367
  92.6 0.1 reverse_bitcast_fusion
  92.7 0.7 copy.16
  93.5 0.0 copy-start.4
  93.5 1.6 %copy-done.4 = bf16[4096,256]{1,0:T(8,128)(2,1)S(1)} copy-done((bf16[4096,256]{1,0:T(8,128)(2,1)S(1)}, bf16[4096,256]{1,0:T(8,128)(2,1)}, u32[]{:S(2)}) %copy-start.4) | copy-done | bytes 2097176
  95.1 7.5 %spatial_back.1 = bf16[4096,256]{1,0:T(8,128)(2,1)} custom-call(bf16[4096,256]{1,0:T(8,128)(2,1)S(1)} %copy-done.4, bf16[3,768,256]{2,1,0:T(8,128)(2,1)S(1)} %bitcast.21), custom_call_target="tpu_custom_call" | custom-call | flops 4831838208 | bytes 4194304 | tf_op jit(solution)/shard_map/spatial_back/pallas_call | solution.py:306
  102.5 5.9 %all-to-all-done.1.parts = bf16[64,24,256]{2,1,0:T(8,128)(2,1)S(1)} async-done(((bf16[64,24,256]{2,1,0:T(8,128)(2,1)}), bf16[64,24,256]{2,1,0:T(8,128)(2,1)S(1)}, u32[]{:S(2)}, u32[]{:S(2)}) %all-to-all-start.1) | async-done | bytes 786464 | tf_op jit(solution)/shard_map/all_to_all | solution.py:367
  108.4 0.1 total.1
  108.6 13.8 %all_to_all.15 = bf16[32,24,256]{2,1,0:T(8,128)(2,1)S(1)} all-to-all(bf16[32,24,256]{2,1,0:T(8,128)(2,1)S(1)} %total.1), channel_id=1, replica_groups=mesh['clip'=32,'half'=2,'core'=2] {'clip'}, dimensions={0} | all-to-all | bytes 786432 | tf_op jit(solution)/shard_map/all_to_all | solution.py:367
  122.3 0.9 turn.1
Async XLA Ops:
  3.7 9.6 %copy-start.6 = (s32[32]{0:T(128)S(1)}, s32[32]{0:T(128)}, u32[]{:S(2)}) copy-start(s32[32]{0:T(128)} %times.1) | copy-start | bytes 388
  3.7 10.2 %copy-start = (bf16[1,1,64,64,256]{4,3,2,1,0:T(8,128)(2,1)S(1)}, bf16[1,1,64,64,256]{4,3,2,1,0:T(8,128)(2,1)}, u32[]{:S(2)}) copy-start(bf16[1,1,64,64,256]{4,3,2,1,0:T(8,128)(2,1)} %param.5) | copy-start | bytes 6291460
  3.7 63.7 %all-to-all-start = ((bf16[32,2,128,256]{3,2,1,0:T(8,128)(2,1)}), bf16[32,2,128,256]{3,2,1,0:T(8,128)(2,1)}, u32[]{:S(2)}, u32[]{:S(2)}) async-start(bf16[32,2,128,256]{3,2,1,0:T(8,128)(2,1)} %spread.1), calls=%async_computation | async-start | bytes 8388608 | tf_op jit(solution)/shard_map/all_to_all | solution.py:367
  14.0 3.0 %copy-start.2 = (bf16[3,3,256,256]{3,2,1,0:T(8,128)(2,1)S(1)}, bf16[3,3,256,256]{3,2,1,0:T(8,128)(2,1)}, u32[]{:S(2)}) copy-start(bf16[3,3,256,256]{3,2,1,0:T(8,128)(2,1)} %param.6) | copy-start | bytes 3538948
  24.2 1.3 %copy-start.1 = (bf16[4096,256]{1,0:T(8,128)(2,1)}, bf16[4096,256]{1,0:T(8,128)(2,1)S(1)}, u32[]{:S(2)}) copy-start(bf16[4096,256]{1,0:T(8,128)(2,1)S(1)} %get-tuple-element.13) | copy-start | bytes 6291460
  25.5 2.0 %copy-start.3 = (f32[4096,256]{1,0:T(8,128)}, f32[4096,256]{1,0:T(8,128)S(1)}, u32[]{:S(2)}) copy-start(f32[4096,256]{1,0:T(8,128)S(1)} %get-tuple-element.12.slope_in) | copy-start | bytes 12582916
  27.5 6.2 %copy-start.5 = (bf16[4096,256]{0,1:T(8,128)(2,1)S(1)}, bf16[4096,256]{0,1:T(8,128)(2,1)}, u32[]{:S(2)}) copy-start(bf16[4096,256]{0,1:T(8,128)(2,1)} %copy.14) | copy-start | bytes 6291460
  78.9 2.4 %collective-permute-start = (bf16[1536,256]{1,0:T(8,128)(2,1)S(1)}, bf16[1536,256]{1,0:T(8,128)(2,1)S(1)}, u32[]{:S(2)}, u32[]{:S(2)}) collective-permute-start(bf16[1536,256]{1,0:T(8,128)(2,1)S(1)} %get-tuple-element.15), channel_id=1, source_target_pairs={{0,1},{1,0},{2,3},{3,2},{4,5},{5,4},{6,7},{7,6},{8,9},{9,8},{10,11... | collective-permute-start | bytes 2359304 | tf_op jit(solution)/shard_map/ppermute | solution.py:389
  82.5 26.0 %all-to-all-start.1 = ((bf16[64,24,256]{2,1,0:T(8,128)(2,1)}), bf16[64,24,256]{2,1,0:T(8,128)(2,1)S(1)}, u32[]{:S(2)}, u32[]{:S(2)}) async-start(bf16[64,24,256]{2,1,0:T(8,128)(2,1)} %bitcast.24), calls=%async_computation.1 | async-start | bytes 1572864 | tf_op jit(solution)/shard_map/all_to_all | solution.py:367
  93.5 1.6 %copy-start.4 = (bf16[4096,256]{1,0:T(8,128)(2,1)S(1)}, bf16[4096,256]{1,0:T(8,128)(2,1)}, u32[]{:S(2)}) copy-start(bf16[4096,256]{1,0:T(8,128)(2,1)} %get-tuple-element.16.hidden_grad) | copy-start | bytes 6291460

commit v6 on v5

--- a/solution.py
+++ b/solution.py
@@ -94,10 +94,10 @@
 
 def side_by_side(block, width):
     rows, chans = block.shape
-    wide = block.astype(F32)
     col = lax.broadcasted_iota(jnp.int32, (rows, chans), 0) & (width - 1)
-    left = jnp.where(col == 0, 0.0, pltpu.roll(wide, 1, 0)).astype(BF16)
-    right = jnp.where(col == width - 1, 0.0, pltpu.roll(wide, rows - 1, 0)).astype(BF16)
+    none = jnp.zeros((), BF16)
+    left = jnp.where(col == 0, none, pltpu.roll(block, 1, 0))
+    right = jnp.where(col == width - 1, none, pltpu.roll(block, rows - 1, 0))
     return left, block, right
 
 

time: 124 us -> 124 us (level)
  no operation moved by 1% of the time
where the time goes in v6:
time: 124 us; the launch traced here: 123 us
  waiting for transfers between devices  38.5 us (31%)
  Pallas kernels  30.6 us (25%)
  starting transfers between devices  19.8 us (16%)
  local copies, waits for them, and re-layouts  17.8 us (14%)
  blocking collectives  13.8 us (11%)
  other arithmetic  1.9 us (2%)
    all_to_all x2, waiting for transfers between devices, exchange(): return lax.all_to_all(x, axes, split_axis=0, concat_axis=0, tiled=True)  36.3 us
    all_to_all x2, starting transfers between devices, exchange(): return lax.all_to_all(x, axes, split_axis=0, concat_axis=0, tiled=True)  19.7 us
    all_to_all x1, blocking collectives, exchange(): return lax.all_to_all(x, axes, split_axis=0, concat_axis=0, tiled=True)  13.8 us
    pallas_call x1, Pallas kernels, filter_call(): pl.pallas_call(functools.partial(filter_kernel, width, cuts), out_shape=(...  11.5 us
    pallas_call x1, Pallas kernels, back_call(): pl.pallas_call(functools.partial(back_kernel, width), grid=(steps,), out_...  7.65 us
    pallas_call x1, Pallas kernels, forward_call(): pl.pallas_call(functools.partial(forward_kernel, width), grid=(steps,), o...  7.4 us
    unnamed x15, local copies, waits for them, and re-layouts  6.8 us
    pallas_call x1, local copies, waits for them, and re-layouts, forward_call(): pl.pallas_call(functools.partial(forward_kernel, width), grid=(steps,), o...  4.27 us
  transfers between devices with their start and end apart: 3, of which 3 were waited for; matrix products, arithmetic and copies ran while one was open for 11% of the time, Pallas kernels for 12%

profile of v6, /device:TPU:0, one launch (start us, length us, event | category | flops | bytes accessed | tf_op | source)
XLA Modules:
  0.0 123.2 jit_solution(5406160758963877384)
XLA Ops:
  0.6 3.0 %spread.1 = bf16[32,2,128,256]{3,2,1,0:T(8,128)(2,1)} custom-call(s32[32]{0:T(128)} %times.1, bf16[16,128,256]{2,1,0:T(8,128)(2,1)} %bitcast.26), custom_call_target="tpu_custom_call" | custom-call | bytes 5242880 | tf_op jit(solution)/shard_map/spread/pallas_call | solution.py:77
  3.6 0.0 copy-start.6
  3.6 0.0 copy-start
  3.7 9.5 %all-to-all-start = ((bf16[32,2,128,256]{3,2,1,0:T(8,128)(2,1)}), bf16[32,2,128,256]{3,2,1,0:T(8,128)(2,1)}, u32[]{:S(2)}, u32[]{:S(2)}) async-start(bf16[32,2,128,256]{3,2,1,0:T(8,128)(2,1)} %spread.1), calls=%async_computation | async-start | bytes 8388608 | tf_op jit(solution)/shard_map/all_to_all | solution.py:367
  13.2 0.0 copy-done.6
  13.2 0.7 dynamic_slice.3
  13.9 0.0 copy-done
  13.9 0.0 copy-start.2
  13.9 3.0 %copy.14 = bf16[4096,256]{0,1:T(8,128)(2,1)} copy(bf16[4096,256]{1,0:T(8,128)(2,1)S(1)} %bitcast.17) | data formatting | bytes 4194304 | tf_op jit(solution)/shard_map/reshape | solution.py:377
  16.9 0.0 copy-done.2
  16.9 7.4 %spatial_forward.1 = (bf16[4096,256]{1,0:T(8,128)(2,1)S(1)}, f32[4096,256]{1,0:T(8,128)S(1)}) custom-call(bf16[4096,256]{1,0:T(8,128)(2,1)S(1)} %bitcast.18, bf16[3,768,256]{2,1,0:T(8,128)(2,1)S(1)} %bitcast.20), custom_call_target="tpu_custom_call" | custom-call | flops 4831838208 | bytes 8388608 | tf_op jit(solution)/shard_map/spatial_forward/pallas_call | solution.py:141
  24.3 0.0 copy-start.1
  24.3 1.3 %copy-done.1 = bf16[4096,256]{1,0:T(8,128)(2,1)} copy-done((bf16[4096,256]{1,0:T(8,128)(2,1)}, bf16[4096,256]{1,0:T(8,128)(2,1)S(1)}, u32[]{:S(2)}) %copy-start.1) | copy-done | bytes 2097176
  25.6 0.0 copy-start.3
  25.6 2.0 %copy-done.3 = f32[4096,256]{1,0:T(8,128)} copy-done((f32[4096,256]{1,0:T(8,128)}, f32[4096,256]{1,0:T(8,128)S(1)}, u32[]{:S(2)}) %copy-start.3) | copy-done | bytes 4194328
  27.6 0.0 copy-start.5
  27.6 4.3 %copy.13 = bf16[4096,256]{0,1:T(8,128)(2,1)} copy(bf16[4096,256]{1,0:T(8,128)(2,1)} %copy-done.1) | data formatting | bytes 4194304 | tf_op jit(solution)/shard_map/spatial_forward/pallas_call | solution.py:141
  31.9 1.9 %copy.15 = bf16[3,256,256]{1,2,0:T(8,128)(2,1)} copy(bf16[3,256,256]{2,1,0:T(8,128)(2,1)} %param.7) | data formatting | bytes 786432 | tf_op args[2]
  33.8 0.0 copy-done.5
  33.8 2.2 %pad.4.padded_in = bf16[256,4224]{1,0:T(8,128)(2,1)} pad(bf16[256,4096]{1,0:T(8,128)(2,1)S(1)} %bitcast.23, bf16[]{:T(256)} %constant.17.clone.1), padding=0_0x64_64 | pad | bytes 4259842 | tf_op jit(solution)/shard_map/jit(_pad)/pad | solution.py:381
  36.0 0.8 pad_add_fusion.place
  36.8 30.6 %all-to-all-done.recv = bf16[32,2,128,256]{3,2,1,0:T(8,128)(2,1)} async-done(((bf16[32,2,128,256]{3,2,1,0:T(8,128)(2,1)}), bf16[32,2,128,256]{3,2,1,0:T(8,128)(2,1)}, u32[]{:S(2)}, u32[]{:S(2)}) %all-to-all-start) | async-done | bytes 4194336 | tf_op jit(solution)/shard_map/all_to_all | solution.py:367
  67.3 11.5 %filters.1 = (bf16[4096,256]{1,0:T(8,128)(2,1)}, f32[1536,256]{1,0:T(8,128)S(1)}, bf16[1536,256]{1,0:T(8,128)(2,1)S(1)}) custom-call(s32[3]{0:T(128)S(1)} %pad_add_fusion.place, bf16[32,2,128,256]{3,2,1,0:T(8,128)(2,1)} %all-to-all-done.recv, f32[4096,256]{1,0:T(8,128)} %copy-done.3, bf16[256,4096]{1,0:T(8,128)(2,1)} %bitcast.25, ...), custom_call_target="tpu_custom_call" | custom-call | flops 6979321856 | bytes 18874368 | tf_op jit(solution)/shard_map/filters/pallas_call | solution.py:249
  78.8 0.1 collective-permute-start
  78.9 2.3 %collective-permute-done = bf16[1536,256]{1,0:T(8,128)(2,1)S(1)} collective-permute-done((bf16[1536,256]{1,0:T(8,128)(2,1)S(1)}, bf16[1536,256]{1,0:T(8,128)(2,1)S(1)}, u32[]{:S(2)}, u32[]{:S(2)}) %collective-permute-start) | collective-permute-done | bytes 786464 | tf_op jit(solution)/shard_map/ppermute | solution.py:389
  81.2 1.1 add_convert_fusion
  82.4 10.2 %all-to-all-start.1 = ((bf16[64,24,256]{2,1,0:T(8,128)(2,1)}), bf16[64,24,256]{2,1,0:T(8,128)(2,1)S(1)}, u32[]{:S(2)}, u32[]{:S(2)}) async-start(bf16[64,24,256]{2,1,0:T(8,128)(2,1)} %bitcast.24), calls=%async_computation.1 | async-start | bytes 1572864 | tf_op jit(solution)/shard_map/all_to_all | solution.py:367
  92.5 0.1 reverse_bitcast_fusion
  92.6 0.7 copy.16
  93.4 0.0 copy-start.4
  93.4 1.6 %copy-done.4 = bf16[4096,256]{1,0:T(8,128)(2,1)S(1)} copy-done((bf16[4096,256]{1,0:T(8,128)(2,1)S(1)}, bf16[4096,256]{1,0:T(8,128)(2,1)}, u32[]{:S(2)}) %copy-start.4) | copy-done | bytes 2097176
  95.0 7.7 %spatial_back.1 = bf16[4096,256]{1,0:T(8,128)(2,1)} custom-call(bf16[4096,256]{1,0:T(8,128)(2,1)S(1)} %copy-done.4, bf16[3,768,256]{2,1,0:T(8,128)(2,1)S(1)} %bitcast.21), custom_call_target="tpu_custom_call" | custom-call | flops 4831838208 | bytes 4194304 | tf_op jit(solution)/shard_map/spatial_back/pallas_call | solution.py:306
  102.6 5.7 %all-to-all-done.1.parts = bf16[64,24,256]{2,1,0:T(8,128)(2,1)S(1)} async-done(((bf16[64,24,256]{2,1,0:T(8,128)(2,1)}), bf16[64,24,256]{2,1,0:T(8,128)(2,1)S(1)}, u32[]{:S(2)}, u32[]{:S(2)}) %all-to-all-start.1) | async-done | bytes 786464 | tf_op jit(solution)/shard_map/all_to_all | solution.py:367
  108.3 0.1 total.1
  108.5 13.8 %all_to_all.15 = bf16[32,24,256]{2,1,0:T(8,128)(2,1)S(1)} all-to-all(bf16[32,24,256]{2,1,0:T(8,128)(2,1)S(1)} %total.1), channel_id=1, replica_groups=mesh['clip'=32,'half'=2,'core'=2] {'clip'}, dimensions={0} | all-to-all | bytes 786432 | tf_op jit(solution)/shard_map/all_to_all | solution.py:367
  122.2 0.9 turn.1
Async XLA Ops:
  3.6 9.6 %copy-start.6 = (s32[32]{0:T(128)S(1)}, s32[32]{0:T(128)}, u32[]{:S(2)}) copy-start(s32[32]{0:T(128)} %times.1) | copy-start | bytes 388
  3.6 10.2 %copy-start = (bf16[1,1,64,64,256]{4,3,2,1,0:T(8,128)(2,1)S(1)}, bf16[1,1,64,64,256]{4,3,2,1,0:T(8,128)(2,1)}, u32[]{:S(2)}) copy-start(bf16[1,1,64,64,256]{4,3,2,1,0:T(8,128)(2,1)} %param.5) | copy-start | bytes 6291460
  3.7 63.7 %all-to-all-start = ((bf16[32,2,128,256]{3,2,1,0:T(8,128)(2,1)}), bf16[32,2,128,256]{3,2,1,0:T(8,128)(2,1)}, u32[]{:S(2)}, u32[]{:S(2)}) async-start(bf16[32,2,128,256]{3,2,1,0:T(8,128)(2,1)} %spread.1), calls=%async_computation | async-start | bytes 8388608 | tf_op jit(solution)/shard_map/all_to_all | solution.py:367
  13.9 3.0 %copy-start.2 = (bf16[3,3,256,256]{3,2,1,0:T(8,128)(2,1)S(1)}, bf16[3,3,256,256]{3,2,1,0:T(8,128)(2,1)}, u32[]{:S(2)}) copy-start(bf16[3,3,256,256]{3,2,1,0:T(8,128)(2,1)} %param.6) | copy-start | bytes 3538948
  24.3 1.3 %copy-start.1 = (bf16[4096,256]{1,0:T(8,128)(2,1)}, bf16[4096,256]{1,0:T(8,128)(2,1)S(1)}, u32[]{:S(2)}) copy-start(bf16[4096,256]{1,0:T(8,128)(2,1)S(1)} %get-tuple-element.13) | copy-start | bytes 6291460
  25.6 2.0 %copy-start.3 = (f32[4096,256]{1,0:T(8,128)}, f32[4096,256]{1,0:T(8,128)S(1)}, u32[]{:S(2)}) copy-start(f32[4096,256]{1,0:T(8,128)S(1)} %get-tuple-element.12.slope_in) | copy-start | bytes 12582916
  27.6 6.2 %copy-start.5 = (bf16[4096,256]{0,1:T(8,128)(2,1)S(1)}, bf16[4096,256]{0,1:T(8,128)(2,1)}, u32[]{:S(2)}) copy-start(bf16[4096,256]{0,1:T(8,128)(2,1)} %copy.14) | copy-start | bytes 6291460
  78.8 2.4 %collective-permute-start = (bf16[1536,256]{1,0:T(8,128)(2,1)S(1)}, bf16[1536,256]{1,0:T(8,128)(2,1)S(1)}, u32[]{:S(2)}, u32[]{:S(2)}) collective-permute-start(bf16[1536,256]{1,0:T(8,128)(2,1)S(1)} %get-tuple-element.15), channel_id=1, source_target_pairs={{0,1},{1,0},{2,3},{3,2},{4,5},{5,4},{6,7},{7,6},{8,9},{9,8},{10,11... | collective-permute-start | bytes 2359304 | tf_op jit(solution)/shard_map/ppermute | solution.py:389
  82.4 26.0 %all-to-all-start.1 = ((bf16[64,24,256]{2,1,0:T(8,128)(2,1)}), bf16[64,24,256]{2,1,0:T(8,128)(2,1)S(1)}, u32[]{:S(2)}, u32[]{:S(2)}) async-start(bf16[64,24,256]{2,1,0:T(8,128)(2,1)} %bitcast.24), calls=%async_computation.1 | async-start | bytes 1572864 | tf_op jit(solution)/shard_map/all_to_all | solution.py:367
  93.4 1.6 %copy-start.4 = (bf16[4096,256]{1,0:T(8,128)(2,1)S(1)}, bf16[4096,256]{1,0:T(8,128)(2,1)}, u32[]{:S(2)}) copy-start(bf16[4096,256]{1,0:T(8,128)(2,1)} %get-tuple-element.16.hidden_grad) | copy-start | bytes 6291460
